TPU v7x, 32 devices: a whole 2x2x4 slice. The times are simulated.
32 devices in a mesh: seq: 8 (over z, y), rep: 4 (over x, core).
Axes of the slice: x: 2, y: 2, z: 4, core: 2. Of those that a mesh axis runs over, the one named last changes fastest.
Arguments:
- inputs: bfloat16 [64, 512, 512], P('rep', 'seq'), may hold values from -6 to 6
- cotangent: bfloat16 [64, 512, 512], P('rep', 'seq'), may hold values from -6 to 6
- segments: int32 [64, 512], P('rep', 'seq'), may hold values from 0 to 511, as said below
- owners: int32 [24], replicated, may hold values from 0 to 23, each once
- weights: float32 [512, 24, 256], P('seq', 'rep'), may hold values from -0.25 to 0.25
- left_bases: float32 [24, 512, 512], P('rep'), as said below
- right_bases: float32 [24, 256, 256], P('rep'), as said below
- moment_one: float32 [512, 24, 256], P('seq', 'rep')
- moment_two: float32 [512, 24, 256], P('seq', 'rep'), as said below
- norm_params: float32 [4, 512], replicated
- norm_one: float32 [4, 512], replicated
- norm_two: float32 [4, 512], replicated, as said below
- positions: float32 [512, 512], replicated, may hold values from -3 to 3
- pos_one: float32 [512, 512], replicated
- pos_two: float32 [512, 512], replicated, as said below
Outputs:
- result: bfloat16 [64, 512, 512], P('rep', 'seq')
- input_grad: float32 [64, 512, 512], P('rep', 'seq')
- new_moment_one: float32 [512, 24, 256], P('seq', 'rep')
- new_moment_two: float32 [512, 24, 256], P('seq', 'rep')
- new_weights: float32 [512, 24, 256], P('seq', 'rep')
- new_norm_one: float32 [4, 512], replicated
- new_norm_two: float32 [4, 512], replicated
- new_norms: float32 [4, 512], replicated
- new_pos_one: float32 [512, 512], replicated
- new_pos_two: float32 [512, 512], replicated
- new_positions: float32 [512, 512], replicated
Inputs may be any that keep to these rules, and one draw needn't show every extreme that they name: `segments`: each row starts at document 0 and its numbers never fall, by at most one from a character to the next; in each aligned block of 16 rows one row is a single document and another has a new document at every character. `owners`: each slot holds exactly one tile. `left_bases`: each slot's basis is orthogonal. `right_bases`: each slot's basis is orthogonal. `moment_two`: all entries are positive. `norm_two`: all entries are positive. `pos_two`: all entries are positive.
All inputs are finite; a program needn't handle non-finite values.
Results may differ from a plain program's by a relative error of at most 0.015.
Values may be sent and summed in bfloat16 or wider, within the bound.
No kernel may reach another device: no remote copies, remote signals or barrier semaphores. Data moves between devices by JAX's collectives and lax.ppermute only.
A program may use at most 192 MiB of HBM per device.

v0:
```python
import jax
import jax.numpy as jnp
from jax import lax
from jax.sharding import PartitionSpec as P

H = 8
WIN = 512
STEP = 10


EPS_NORM = 1e-05
EPS_ADAM = 1e-08
BETA = 0.5
LEARN = 0.02
LEARN_SMALL = 0.2
DECAY = 0.01
MASKED = -1e30
HIGH_PRECISION = lax.Precision.HIGHEST


def split_tiles(query_key_value_weight, output_weight, up_weight, down_weight):
    model_width = query_key_value_weight.shape[0]
    half_width = model_width // 2
    blocks = down_weight.shape[0] // model_width
    down_tiles = (
        down_weight.reshape(blocks, model_width, 2, half_width)
        .transpose(1, 0, 2, 3)
        .reshape(model_width, 2 * blocks, half_width)
    )
    return jnp.concatenate(
        [
            query_key_value_weight.reshape(model_width, -1, half_width),
            output_weight.reshape(model_width, -1, half_width),
            up_weight.reshape(model_width, -1, half_width),
            down_tiles,
        ],
        axis=1,
    )


def join_tiles(tile_stack):
    model_width, count_all, half_width = tile_stack.shape
    hidden = (count_all - 8) * model_width // 4
    up_count = 2 * hidden // model_width
    blocks = hidden // model_width
    query_key_value_weight = tile_stack[:, 0:6].reshape(model_width, 3 * model_width)
    output_weight = tile_stack[:, 6:8].reshape(model_width, model_width)
    up_weight = tile_stack[:, 8 : 8 + up_count].reshape(model_width, hidden)
    down_weight = (
        tile_stack[:, 8 + up_count :]
        .reshape(model_width, blocks, 2, half_width)
        .transpose(1, 0, 2, 3)
        .reshape(hidden, model_width)
    )
    return (query_key_value_weight, output_weight, up_weight, down_weight)


def adam_step(gradient, first, second):
    first_new = BETA * first + (1.0 - BETA) * gradient
    second_new = BETA * second + (1.0 - BETA) * gradient * gradient
    fix = 1.0 - BETA**STEP
    direction = first_new / fix / (jnp.sqrt(second_new / fix) + EPS_ADAM)
    return (first_new, second_new, direction)


def norm_forward(values, gain, shift):
    center = values - jnp.mean(values, axis=-1, keepdims=True)
    inverse = lax.rsqrt(jnp.mean(center * center, axis=-1, keepdims=True) + EPS_NORM)
    scaled = center * inverse
    return (scaled * gain + shift, scaled, inverse)


def norm_backward(grad_rows, scaled, inverse, gain):
    grad_gain = jnp.sum(grad_rows * scaled, axis=0)
    grad_shift = jnp.sum(grad_rows, axis=0)
    scaled_grad = grad_rows * gain
    grad_input = inverse * (
        scaled_grad
        - jnp.mean(scaled_grad, axis=-1, keepdims=True)
        - scaled * jnp.mean(scaled_grad * scaled, axis=-1, keepdims=True)
    )
    return (grad_input, grad_gain, grad_shift)


def window_scores(qkv_win, ids_win, head_dim):
    query = qkv_win[..., :head_dim]
    keys_all = qkv_win[..., head_dim : 2 * head_dim]
    scores = jnp.einsum(
        "pqe,pke->pqk", query, keys_all, preferred_element_type=jnp.float32
    ) * head_dim ** (-0.5)
    causal = jnp.arange(qkv_win.shape[1])[:, None] >= jnp.arange(qkv_win.shape[1])[None, :]
    allowed = (ids_win[:, :, None] == ids_win[:, None, :]) & causal[None]
    return jnp.where(allowed, scores, MASKED)


def attend_forward(by_head, pair_ids):
    pair_count, length, triple = by_head.shape
    head_dim = triple // 3

    def one_window(window, buffers):
        outputs, log_sums = buffers
        qkv_win = lax.dynamic_slice_in_dim(by_head, window * WIN, WIN, 1)
        ids_win = lax.dynamic_slice_in_dim(pair_ids, window * WIN, WIN, 1)
        masked = window_scores(qkv_win, ids_win, head_dim)
        highest = jnp.max(masked, axis=-1, keepdims=True)
        powers = jnp.exp(masked - highest)
        totals = jnp.sum(powers, axis=-1, keepdims=True)
        probs = (powers / totals).astype(jnp.bfloat16)
        mixed_heads = jnp.einsum(
            "pqk,pke->pqe", probs, qkv_win[..., 2 * head_dim :], preferred_element_type=jnp.float32
        ).astype(jnp.bfloat16)
        outputs = lax.dynamic_update_slice_in_dim(outputs, mixed_heads, window * WIN, 1)
        log_sums = lax.dynamic_update_slice_in_dim(
            log_sums, (highest + jnp.log(totals))[..., 0], window * WIN, 1
        )
        return (outputs, log_sums)

    initial = (
        jnp.zeros((pair_count, length, head_dim), jnp.bfloat16),
        jnp.zeros((pair_count, length), jnp.float32),
    )
    return lax.fori_loop(0, length // WIN, one_window, initial)


def attend_backward(by_head, log_sums, grad_head, pair_ids):
    pair_count, length, triple = by_head.shape
    head_dim = triple // 3
    factor = head_dim ** (-0.5)

    def one_window(window, grad_buffer):
        qkv_win = lax.dynamic_slice_in_dim(by_head, window * WIN, WIN, 1)
        ids_win = lax.dynamic_slice_in_dim(pair_ids, window * WIN, WIN, 1)
        lse_win = lax.dynamic_slice_in_dim(log_sums, window * WIN, WIN, 1)
        grad_win = lax.dynamic_slice_in_dim(grad_head, window * WIN, WIN, 1)
        masked = window_scores(qkv_win, ids_win, head_dim)
        probs = jnp.exp(masked - lse_win[..., None])
        query = qkv_win[..., :head_dim]
        keys_all = qkv_win[..., head_dim : 2 * head_dim]
        values = qkv_win[..., 2 * head_dim :]
        grad_probs = jnp.einsum(
            "pqe,pke->pqk", grad_win, values, preferred_element_type=jnp.float32
        )
        inner = jnp.sum(probs * grad_probs, axis=-1, keepdims=True)
        grad_scores = (probs * (grad_probs - inner)).astype(jnp.bfloat16)
        grad_query = (
            jnp.einsum("pqk,pke->pqe", grad_scores, keys_all, preferred_element_type=jnp.float32)
            * factor
        )
        grad_keys = (
            jnp.einsum("pqk,pqe->pke", grad_scores, query, preferred_element_type=jnp.float32)
            * factor
        )
        grad_values = jnp.einsum(
            "pqk,pqe->pke", probs.astype(jnp.bfloat16), grad_win, preferred_element_type=jnp.float32
        )
        packed = jnp.concatenate([grad_query, grad_keys, grad_values], axis=-1).astype(jnp.bfloat16)
        return lax.dynamic_update_slice_in_dim(grad_buffer, packed, window * WIN, 1)

    return lax.fori_loop(
        0, length // WIN, one_window, jnp.zeros((pair_count, length, triple), jnp.bfloat16)
    )


def body(
    inputs,
    cotangent,
    segments,
    owners,
    weights,
    left_bases,
    right_bases,
    moment_one,
    moment_two,
    norm_params,
    norm_one,
    norm_two,
    positions,
    pos_one,
    pos_two,
):
    seq_count = lax.axis_size("seq")
    seq_index = lax.axis_index("seq")
    seq_local, span, model_width = inputs.shape
    head_dim = model_width // H
    row_count = seq_local * span
    pair_count = seq_local * H // seq_count
    rows_dev = model_width // seq_count
    gathered = lax.all_gather(weights.astype(jnp.bfloat16), "seq", axis=0, tiled=True)
    gathered = lax.all_gather(gathered, "rep", axis=1, tiled=True)
    query_key_value_weight, output_weight, up_weight, down_weight = join_tiles(
        gathered[:, owners, :]
    )
    w_heads = query_key_value_weight.reshape(model_width, H, 3 * head_dim)
    out_heads = output_weight.reshape(H, head_dim, model_width)
    offset = seq_index * span % WIN
    pos_rows = lax.dynamic_slice_in_dim(positions, offset, span, 0)
    all_ids = lax.all_gather(segments, "seq", axis=1, tiled=True)
    hidden_residual_sum = inputs.astype(jnp.float32) + pos_rows[None]
    low_hidden = hidden_residual_sum.astype(jnp.bfloat16)
    projected_output = jnp.einsum(
        "scd,dhe->shce", low_hidden, w_heads, preferred_element_type=jnp.float32
    ).astype(jnp.bfloat16)
    pair_ids = all_ids[(seq_index * pair_count + jnp.arange(pair_count)) // H]
    by_head = lax.all_to_all(
        projected_output.reshape(seq_local * H, span, 3 * head_dim),
        "seq",
        split_axis=0,
        concat_axis=1,
        tiled=True,
    )
    attended, log_sums = attend_forward(by_head, pair_ids)
    returned = lax.all_to_all(attended, "seq", split_axis=1, concat_axis=0, tiled=True).reshape(
        seq_local, H, span, head_dim
    )
    attention_output = jnp.einsum(
        "shce,hed->scd", returned, out_heads, preferred_element_type=jnp.float32
    ).reshape(row_count, model_width)
    first_normed_input, scaled_first, inverse_first = norm_forward(
        hidden_residual_sum.reshape(row_count, model_width) + attention_output,
        norm_params[0],
        norm_params[1],
    )
    low_normed = first_normed_input.astype(jnp.bfloat16)
    preactivation_hidden = jnp.dot(low_normed, up_weight, preferred_element_type=jnp.float32)
    act_low = jax.nn.gelu(preactivation_hidden).astype(jnp.bfloat16)
    branch_output = jnp.dot(act_low, down_weight, preferred_element_type=jnp.float32)
    result, scaled_second, inverse_second = norm_forward(
        first_normed_input + branch_output, norm_params[2], norm_params[3]
    )
    grad_final = cotangent.astype(jnp.float32).reshape(row_count, model_width)
    grad_resid, gain_two, shift_two = norm_backward(
        grad_final, scaled_second, inverse_second, norm_params[2]
    )
    grad_branch = grad_resid.astype(jnp.bfloat16)
    grad_down = jnp.einsum("rf,rd->fd", act_low, grad_branch, preferred_element_type=jnp.float32)
    grad_act = jnp.einsum("rd,fd->rf", grad_branch, down_weight, preferred_element_type=jnp.float32)
    gelu_pull = jax.vjp(jax.nn.gelu, preactivation_hidden)[1]
    grad_pre = gelu_pull(grad_act)[0].astype(jnp.bfloat16)
    grad_up = jnp.einsum("rd,rf->df", low_normed, grad_pre, preferred_element_type=jnp.float32)
    grad_normed = grad_resid + jnp.einsum(
        "rf,df->rd", grad_pre, up_weight, preferred_element_type=jnp.float32
    )
    grad_mid, gain_one, shift_one = norm_backward(
        grad_normed, scaled_first, inverse_first, norm_params[0]
    )
    grad_attn = grad_mid.astype(jnp.bfloat16).reshape(seq_local, span, model_width)
    grad_out = jnp.einsum(
        "shce,scd->hed", returned, grad_attn, preferred_element_type=jnp.float32
    ).reshape(model_width, model_width)
    grad_mixed = jnp.einsum(
        "scd,hed->shce", grad_attn, out_heads, preferred_element_type=jnp.float32
    ).astype(jnp.bfloat16)
    grad_by_head = lax.all_to_all(
        grad_mixed.reshape(seq_local * H, span, head_dim),
        "seq",
        split_axis=0,
        concat_axis=1,
        tiled=True,
    )
    grad_packed = attend_backward(by_head, log_sums, grad_by_head, pair_ids)
    grad_proj = lax.all_to_all(grad_packed, "seq", split_axis=1, concat_axis=0, tiled=True).reshape(
        seq_local, H, span, 3 * head_dim
    )
    grad_qkv = jnp.einsum(
        "scd,shce->dhe", low_hidden, grad_proj, preferred_element_type=jnp.float32
    ).reshape(model_width, 3 * model_width)
    grad_input = grad_mid.reshape(seq_local, span, model_width) + jnp.einsum(
        "shce,dhe->scd", grad_proj, w_heads, preferred_element_type=jnp.float32
    )
    grad_pos = lax.dynamic_update_slice_in_dim(
        jnp.zeros(positions.shape, jnp.float32), jnp.sum(grad_input, axis=0), offset, 0
    )
    grad_norms = jnp.stack([gain_one, shift_one, gain_two, shift_two])
    grad_norms, grad_pos = lax.psum((grad_norms, grad_pos), ("seq", "rep"))
    grad_tiles = split_tiles(grad_qkv, grad_out, grad_up, grad_down)
    grad_slots = jnp.zeros_like(grad_tiles).at[:, owners, :].set(grad_tiles)
    partial_sum = lax.psum_scatter(
        grad_slots.astype(jnp.bfloat16), "rep", scatter_dimension=1, tiled=True
    ).astype(jnp.float32)
    leftward = jnp.einsum("sir,isc->rsc", left_bases, partial_sum, precision=HIGH_PRECISION)
    turned = lax.psum_scatter(
        jnp.einsum("rsc,scd->rsd", leftward, right_bases, precision=HIGH_PRECISION).astype(
            jnp.bfloat16
        ),
        "seq",
        scatter_dimension=0,
        tiled=True,
    ).astype(jnp.float32)
    first_new, second_new, direction = adam_step(turned, moment_one, moment_two)
    change = jnp.einsum("rsc,sdc->rsd", direction, right_bases, precision=HIGH_PRECISION)
    own_cols = lax.dynamic_slice_in_dim(left_bases, seq_index * rows_dev, rows_dev, 2)
    mine = lax.psum_scatter(
        jnp.einsum("sir,rsd->isd", own_cols, change, precision=HIGH_PRECISION).astype(jnp.bfloat16),
        "seq",
        scatter_dimension=0,
        tiled=True,
    ).astype(jnp.float32)
    new_weights = weights - LEARN * (mine + DECAY * weights)
    norm_first, norm_second, norm_dir = adam_step(grad_norms, norm_one, norm_two)
    pos_first, pos_second, pos_dir = adam_step(grad_pos, pos_one, pos_two)
    return (
        result.reshape(seq_local, span, model_width).astype(jnp.bfloat16),
        grad_input,
        first_new,
        second_new,
        new_weights,
        norm_first,
        norm_second,
        norm_params - LEARN_SMALL * norm_dir,
        pos_first,
        pos_second,
        positions - LEARN_SMALL * pos_dir,
    )


def solution(mesh):
    return jax.shard_map(
        body,
        mesh=mesh,
        in_specs=(
            P("rep", "seq", None),
            P("rep", "seq", None),
            P("rep", "seq"),
            P(),
            P("seq", "rep", None),
            P("rep", None, None),
            P("rep", None, None),
            P("seq", "rep", None),
            P("seq", "rep", None),
            P(),
            P(),
            P(),
            P(),
            P(),
            P(),
        ),
        out_specs=(
            P("rep", "seq", None),
            P("rep", "seq", None),
            P("seq", "rep", None),
            P("seq", "rep", None),
            P("seq", "rep", None),
            P(),
            P(),
            P(),
            P(),
            P(),
            P(),
        ),
        check_vma=False,
    )
```

profile of v0, /device:TPU:0, one launch (start us, length us, event | category | flops | bytes accessed | tf_op | source)
XLA Modules:
  0.0 958.8 jit_solution(11184923294463037791)
XLA Ops:
  9.1 48.6 %all-gather.4.cloned.1.call-done = bf16[512,6,256]{2,0,1:T(8,128)(2,1)} async-done(((bf16[64,6,256]{2,0,1:T(8,128)(2,1)}), bf16[512,6,256]{2,0,1:T(8,128)(2,1)}) %all-gather.4.cloned.1.call-update) | async-done | bytes 1572880 | tf_op jit(solution)/shard_map/all_gather | solution.py:188
  59.9 44.6 %all-gather.6.cloned.1.call-done = bf16[512,24,256]{2,0,1:T(8,128)(2,1)} async-done(((bf16[512,6,256]{2,0,1:T(8,128)(2,1)}), bf16[512,24,256]{2,0,1:T(8,128)(2,1)}) %all-gather.6.cloned.1.call-update) | async-done | bytes 6291472 | tf_op jit(solution)/shard_map/all_gather | solution.py:189
  104.5 7.2 gather_fusion.1
  126.8 113.7 %all-gather = s32[8,64,16]{1,2,0:T(8,128)S(1)} all-gather(s32[1,64,16]{1,2,0:T(8,128)S(1)} %bitcast.212), channel_id=1, replica_groups=mesh['seq'=8,'rep'=4] {'seq'}, dimensions={0}, use_global_device_ids=true | all-gather | bytes 36864 | tf_op jit(solution)/shard_map/all_gather | solution.py:197
  244.0 9.3 fusion.93
  253.4 8.3 fusion
  261.7 9.3 fusion.42
  334.4 7.2 fusion.8
  365.1 20.4 %all-to-all-done.2 = bf16[8,2,32768]{2,1,0:T(2,128)(2,1)S(1)} async-done(((bf16[8,2,32768]{2,1,0:T(2,128)(2,1)}), bf16[8,2,32768]{2,1,0:T(2,128)(2,1)S(1)}, u32[]{:S(2)}, u32[]{:S(2)}) %all-to-all-start.2) | async-done | bytes 1048608 | tf_op jit(solution)/shard_map/all_to_all | solution.py:253
  395.5 11.4 %multiply_reduce_fusion = (f32[16,512]{1,0:T(8,128)S(1)}, f32[16,512,512]{1,2,0:T(8,128)}) fusion(f32[16,512,512]{1,2,0:T(8,128)} %get-tuple-element.143, f32[16,512]{1,0:T(8,128)S(1)} %log_add_fusion, bf16[16,512,64]{1,2,0:T(8,128)(2,1)S(1)} %all_to_all.58, bf16[16,512,192]{2,1,0:T(8,128)(2,1)} %bitcast.168), kind=kOutput, calls=%fused_computation.4 | convolution fusion | flops 549445632 | bytes 36765696 | tf_op jit(solution)/shard_map/while/body/eval_jaxpr/pqe,pke->pqk/dot_general | solution.py:140
  406.9 11.8 %multiply_convert_fusion = bf16[16,512,512]{1,2,0:T(8,128)(2,1)S(1)} fusion(f32[16,512,512]{1,2,0:T(8,128)} %get-tuple-element.150, f32[16,512,512]{1,2,0:T(8,128)} %get-tuple-element.143, f32[16,512]{1,0:T(8,128)S(1)} %get-tuple-element.149, f32[16,512]{1,0:T(8,128)S(1)} %log_add_fusion), kind=kLoop, calls=%fused_computation.3 | loop fusion | flops 16777216 | bytes 42008576 | tf_op jit(solution)/shard_map/while/body/eval_jaxpr/convert_element_type | solution.py:144
  427.0 9.4 fusion.53
  439.5 7.7 copy.185
  459.9 9.2 fusion.66
  490.2 51.2 %all-to-all-done.3 = bf16[16,512,192]{2,0,1:T(8,128)(2,1)} async-done(((bf16[16,512,192]{2,0,1:T(8,128)(2,1)}), bf16[16,512,192]{2,0,1:T(8,128)(2,1)}, u32[]{:S(2)}, u32[]{:S(2)}) %all-to-all-start.3) | async-done | bytes 3145760 | tf_op jit(solution)/shard_map/all_to_all | solution.py:261
  551.5 8.8 dot_general.107
  576.2 22.8 %scatter_fusion = f32[512,24,256]{2,0,1:T(8,128)} fusion(f32[512,24,256]{2,0,1:T(8,128)} %broadcast_in_dim.36, s32[24]{0:T(128)S(1)} %copy-done.33, f32[24,512,256]{2,1,0:T(8,128)} %maximum_bitcast_fusion), kind=kCustom, calls=%fused_computation.2 | custom fusion | bytes 37748832 | tf_op jit(solution)/shard_map/scatter | solution.py:276
  599.0 8.0 convert_element_type.104
  607.1 56.6 %reduce-scatter.4.cloned.1.call-done = bf16[512,6,256]{2,0,1:T(8,128)(2,1)} async-done(((bf16[512,24,256]{2,0,1:T(8,128)(2,1)}), bf16[512,6,256]{2,0,1:T(8,128)(2,1)}) %reduce-scatter.4.cloned.1.call-update) | async-done | bytes 1572880 | tf_op jit(solution)/shard_map/reduce_scatter | solution.py:277
  663.7 8.9 fusion.97
  686.5 58.2 %reduce-scatter.6.cloned.1.call-done = bf16[64,6,256]{2,0,1:T(8,128)(2,1)} async-done(((bf16[512,6,256]{2,0,1:T(8,128)(2,1)}), bf16[64,6,256]{2,0,1:T(8,128)(2,1)}) %reduce-scatter.6.cloned.1.call-update) | async-done | bytes 196624 | tf_op jit(solution)/shard_map/reduce_scatter | solution.py:281
  757.2 39.9 %psum.14 = f32[4,512]{1,0:T(4,128)S(1)} all-reduce(f32[4,512]{1,0:T(4,128)S(1)} %pad_maximum_fusion.1), channel_id=1, replica_groups=mesh['seq'=8,'rep'=4] {'seq','rep'}, use_global_device_ids=true, to_apply=%region_19.20 | all-reduce | flops 2048 | bytes 16384 | tf_op jit(solution)/shard_map/psum | solution.py:274
  798.4 80.8 %all-reduce.2.cloned.1.call-done = f32[512,512]{1,0:T(8,128)} async-done(((f32[512,512]{1,0:T(8,128)}), f32[512,512]{1,0:T(8,128)}) %all-reduce.2.cloned.1.call-update) | async-done | bytes 1048592 | tf_op jit(solution)/shard_map/psum | solution.py:274
  883.5 66.2 %reduce-scatter.8.cloned.1.call-done = bf16[64,6,256]{2,1,0:T(8,128)(2,1)} async-done(((bf16[512,6,256]{2,1,0:T(8,128)(2,1)}), bf16[64,6,256]{2,1,0:T(8,128)(2,1)}) %reduce-scatter.8.cloned.1.call-update) | async-done | bytes 196624 | tf_op jit(solution)/shard_map/reduce_scatter | solution.py:292
  (173 shorter events, 224.5 us)
Async XLA Ops:
  7.2 665.4 %copy-start = (f32[6,256,256]{2,1,0:T(8,128)S(1)}, f32[6,256,256]{2,1,0:T(8,128)}, u32[]{:S(2)}) copy-start(f32[6,256,256]{2,1,0:T(8,128)} %param.21) | copy-start | bytes 4718596
  7.2 50.5 %all-gather.4.cloned.1.call-start = ((), (), s32[]{:S(2)}) async-start(), calls=%async_computation.7 | async-start | bytes 1769472 | tf_op jit(solution)/shard_map/all_gather | solution.py:188
  9.1 95.4 %all-gather.6.cloned.1.call-start = ((), (), s32[]{:S(2)}) async-start(), calls=%async_computation.8 | async-start | bytes 7864320 | tf_op jit(solution)/shard_map/all_gather | solution.py:189
  59.8 224.1 %copy-start.23 = (f32[64,512]{1,0:T(8,128)}, f32[64,512]{1,0:T(8,128)S(1)}, u32[]{:S(2)}) copy-start(f32[64,512]{1,0:T(8,128)S(1)} %constant_dynamic-slice_fusion) | copy-start | bytes 393220
  121.1 120.1 %all-to-all-start = ((bf16[128,64,192]{2,1,0:T(8,128)(2,1)}), bf16[128,64,192]{2,1,0:T(8,128)(2,1)}, u32[]{:S(2)}, u32[]{:S(2)}) async-start(bf16[128,64,192]{2,1,0:T(8,128)(2,1)} %bitcast.176), calls=%async_computation | async-start | bytes 8388608 | tf_op jit(solution)/shard_map/all_to_all | solution.py:204
  244.0 9.4 copy-start.2
  273.8 8.9 copy-start.27
  273.8 9.0 copy-start.9
  278.3 26.5 %all-to-all-start.1 = ((bf16[8,2,32768]{2,1,0:T(2,128)(2,1)}), bf16[8,2,32768]{2,1,0:T(2,128)(2,1)}, u32[]{:S(2)}, u32[]{:S(2)}) async-start(bf16[8,2,32768]{2,1,0:T(2,128)(2,1)} %reshape.267), calls=%async_computation.1 | async-start | bytes 2097152 | tf_op jit(solution)/shard_map/all_to_all | solution.py:212
  312.6 9.0 copy-start.26
  324.5 20.7 %copy-start.1 = (f32[1024,512]{1,0:T(8,128)}, f32[1024,512]{1,0:T(8,128)S(1)}, u32[]{:S(2)}) copy-start(f32[1024,512]{1,0:T(8,128)S(1)} %get-tuple-element.145) | copy-start | bytes 6291460
  334.4 7.2 copy-start.15
  359.1 26.4 %all-to-all-start.2 = ((bf16[8,2,32768]{2,1,0:T(2,128)(2,1)}), bf16[8,2,32768]{2,1,0:T(2,128)(2,1)S(1)}, u32[]{:S(2)}, u32[]{:S(2)}) async-start(bf16[8,2,32768]{2,1,0:T(2,128)(2,1)} %reshape.269), calls=%async_computation.2 | async-start | bytes 2097152 | tf_op jit(solution)/shard_map/all_to_all | solution.py:253
  406.9 11.9 %copy-start.3 = (bf16[16,8,64,192]{3,2,1,0:T(8,128)(2,1)S(1)}, bf16[16,8,64,192]{3,2,1,0:T(8,128)(2,1)}, u32[]{:S(2)}) copy-start(bf16[16,8,64,192]{3,2,1,0:T(8,128)(2,1)} %copy-done.2) | copy-start | bytes 9437188
  447.2 94.2 %all-to-all-start.3 = ((bf16[16,512,192]{2,0,1:T(8,128)(2,1)}), bf16[16,512,192]{2,0,1:T(8,128)(2,1)}, u32[]{:S(2)}, u32[]{:S(2)}) async-start(bf16[16,512,192]{2,0,1:T(8,128)(2,1)} %copy.185), calls=%async_computation.3 | async-start | bytes 8388608 | tf_op jit(solution)/shard_map/all_to_all | solution.py:261
  451.8 211.9 %reduce-scatter.4.cloned.1.call-start = ((), (), s32[]{:S(2)}) async-start(), calls=%async_computation.9 | async-start | bytes 7864320 | tf_op jit(solution)/shard_map/reduce_scatter | solution.py:277
  551.5 8.8 copy-start.21
  551.5 8.8 copy-start.24
  607.0 137.6 %reduce-scatter.6.cloned.1.call-start = ((), (), s32[]{:S(2)}) async-start(), calls=%async_computation.10 | async-start | bytes 1769472 | tf_op jit(solution)/shard_map/reduce_scatter | solution.py:281
  679.0 200.1 %all-reduce.2.cloned.1.call-start = ((), (), s32[]{:S(2)}) async-start(), calls=%async_computation.12 | async-start | bytes 2097152 | tf_op jit(solution)/shard_map/psum | solution.py:274
  686.2 263.4 %reduce-scatter.8.cloned.1.call-start = ((), (), s32[]{:S(2)}) async-start(), calls=%async_computation.11 | async-start | bytes 2359296 | tf_op jit(solution)/shard_map/reduce_scatter | solution.py:292
  746.0 7.3 copy-start.19
  753.4 43.7 %copy-start.28 = (f32[4,512]{1,0:T(4,128)S(1)}, f32[4,512]{1,0:T(4,128)}, u32[]{:S(2)}) copy-start(f32[4,512]{1,0:T(4,128)} %param.24) | copy-start | bytes 24580
  798.4 151.3 %copy-start.18 = (f32[64,6,256]{2,0,1:T(8,128)S(1)}, f32[64,6,256]{2,0,1:T(8,128)}, u32[]{:S(2)}) copy-start(f32[64,6,256]{2,0,1:T(8,128)} %param.19) | copy-start | bytes 1179652
  (21 other events, 72.4 us)
Sparse Core Ops, SparseCore 0:
  10.8 46.8 all-gather.3
  59.3 45.1 all-gather.5
  607.2 56.4 reduce-scatter.3
  679.1 65.4 reduce-scatter.5
  750.3 128.8 all-reduce.1
  882.9 66.6 reduce-scatter.7
where the time goes:
time: 965 us; the launch traced here: 959 us
  waiting for transfers between devices  427 us (44%)
  local copies, waits for them, and re-layouts  161 us (17%)
  blocking collectives  154 us (16%)
  matrix products  124 us (13%)
  other arithmetic  57.9 us (6%)
  starting transfers between devices  21.5 us (2%)
  between operations  14.9 us (2%)
    all_gather x1, blocking collectives, body(): all_ids = lax.all_gather(segments, 'seq', axis=1, tiled=True)  114 us
    psum x1, waiting for transfers between devices, body(): grad_norms, grad_pos = lax.psum((grad_norms, grad_pos), ('seq', 'rep'))  80.8 us
    reduce_scatter x1, waiting for transfers between devices, body(): lax.psum_scatter(jnp.einsum('sir,rsd->isd', own_cols, change, precision=H...  66.2 us
    reduce_scatter x1, waiting for transfers between devices, body(): lax.psum_scatter(jnp.einsum('rsc,scd->rsd', leftward, right_bases, precis...  58.2 us
    reduce_scatter x1, waiting for transfers between devices, body(): lax.psum_scatter(grad_slots.astype(jnp.bfloat16), 'rep', scatter_dimensio...  56.6 us
    all_to_all x1, waiting for transfers between devices, body(): lax.all_to_all(grad_packed, 'seq', split_axis=1, concat_axis=0, tiled=True)  51.2 us
    all_gather x1, waiting for transfers between devices, body(): lax.all_gather(weights.astype(jnp.bfloat16), 'seq', axis=0, tiled=True)  48.6 us
    all_gather x1, waiting for transfers between devices, body(): gathered = lax.all_gather(gathered, 'rep', axis=1, tiled=True)  44.6 us
  transfers between devices with their start and end apart: 10, of which 8 were waited for; matrix products, arithmetic and copies ran while one was open for 9% of the time, Pallas kernels for 0%

commit v1 on v0

v1 whole, which is shorter than its diff:
```python
import functools

import jax
import jax.numpy as jnp
from jax import lax
from jax.experimental import pallas as pl
from jax.experimental.pallas import tpu as pltpu
from jax.sharding import PartitionSpec as P

H = 8
WIN = 512
STEP = 10

EPS_NORM = 1e-05
EPS_ADAM = 1e-08
BETA = 0.5
LEARN = 0.02
LEARN_SMALL = 0.2
DECAY = 0.01
MASKED = -1e30

BF = jnp.bfloat16
F32 = jnp.float32
VMEM_LIMIT = 58 * 1024 * 1024
GELU_A = 0.7978845608028654
GELU_B = 0.044715


def nn(a, b):
    return lax.dot_general(a, b, (((1,), (0,)), ((), ())), preferred_element_type=F32)


def nt(a, b):
    return lax.dot_general(a, b, (((1,), (1,)), ((), ())), preferred_element_type=F32)


def tn(a, b):
    return lax.dot_general(a, b, (((0,), (0,)), ((), ())), preferred_element_type=F32)


def adam_step(gradient, first, second):
    first_new = BETA * first + (1.0 - BETA) * gradient
    second_new = BETA * second + (1.0 - BETA) * gradient * gradient
    fix = 1.0 - BETA**STEP
    direction = first_new / fix / (jnp.sqrt(second_new / fix) + EPS_ADAM)
    return (first_new, second_new, direction)


def row_norm(values):
    center = values - jnp.mean(values, axis=-1, keepdims=True)
    inverse = lax.rsqrt(jnp.mean(center * center, axis=-1, keepdims=True) + EPS_NORM)
    return center * inverse, inverse


def norm_pull(grad_rows, scaled, inverse, gain):
    scaled_grad = grad_rows * gain
    grad_input = inverse * (
        scaled_grad
        - jnp.mean(scaled_grad, axis=-1, keepdims=True)
        - scaled * jnp.mean(scaled_grad * scaled, axis=-1, keepdims=True)
    )
    grad_gain = jnp.sum(grad_rows * scaled, axis=0, keepdims=True)
    grad_shift = jnp.sum(grad_rows, axis=0, keepdims=True)
    return grad_input, grad_gain, grad_shift


def attend_kernel(x_ref, pos_ref, w_ref, ids_row, ids_col, qkv_ref, mixed_ref, lse_ref, bias):
    win, width = pos_ref.shape
    dim = width // H
    tile = w_ref.shape[2]
    hidden = x_ref[...].reshape(win, width).astype(F32) + pos_ref[...]
    low = hidden.astype(BF)
    for t in range(w_ref.shape[0]):
        qkv_ref[0, :, t * tile : (t + 1) * tile] = nn(low, w_ref[t]).astype(BF)
    row = lax.broadcasted_iota(jnp.int32, (win, win), 0)
    col = lax.broadcasted_iota(jnp.int32, (win, win), 1)
    allowed = (ids_col[0] == ids_row[0]) & (row >= col)
    bias[...] = jnp.where(allowed, 0.0, MASKED)
    half = win // 2
    sums = []
    for pair in range(H // 2):
        outs = []
        for h in (2 * pair, 2 * pair + 1):
            base = 3 * dim * h
            query = qkv_ref[0, :, base : base + dim] * (dim**-0.5)
            keys = qkv_ref[0, :, base + dim : base + 2 * dim]
            values = qkv_ref[0, :, base + 2 * dim : base + 3 * dim]
            parts, logs = [], []
            for lo, count in ((0, half), (half, win)):
                scores = nt(query[lo : lo + half], keys[:count]) + bias[lo : lo + half, :count]
                highest = jnp.max(scores, axis=-1, keepdims=True)
                powers = jnp.exp(scores - highest)
                total = jnp.sum(powers, axis=-1, keepdims=True)
                parts.append(nn(powers.astype(BF), values[:count]) / total)
                logs.append(highest + jnp.log(total))
            outs.append(jnp.concatenate(parts, axis=0))
            sums.append(jnp.concatenate(logs, axis=0))
        mixed_ref[0, :, pair * 2 * dim : (pair + 1) * 2 * dim] = jnp.concatenate(outs, axis=1).astype(BF)
    lanes = jnp.concatenate(sums + [jnp.zeros((win, 128 - H), F32)], axis=1)
    lse_ref[0] = lanes.T[:H]


def attend_forward(x, positions, w_qkv, ids):
    group, wins, span, width = x.shape
    win = group * span
    return pl.pallas_call(
        attend_kernel,
        grid=(wins,),
        in_specs=[
            pl.BlockSpec((group, 1, span, width), lambda i: (0, i, 0, 0)),
            pl.BlockSpec((win, width), lambda i: (0, 0)),
            pl.BlockSpec(w_qkv.shape, lambda i: (0, 0, 0)),
            pl.BlockSpec((1, 1, win), lambda i: (i, 0, 0)),
            pl.BlockSpec((1, win, 1), lambda i: (i, 0, 0)),
        ],
        out_specs=[
            pl.BlockSpec((1, win, 3 * width), lambda i: (i, 0, 0)),
            pl.BlockSpec((1, win, width), lambda i: (i, 0, 0)),
            pl.BlockSpec((1, H, win), lambda i: (i, 0, 0)),
        ],
        out_shape=[
            jax.ShapeDtypeStruct((wins, win, 3 * width), BF),
            jax.ShapeDtypeStruct((wins, win, width), BF),
            jax.ShapeDtypeStruct((wins, H, win), F32),
        ],
        scratch_shapes=[pltpu.VMEM((win, win), F32)],
        compiler_params=pltpu.CompilerParams(vmem_limit_bytes=VMEM_LIMIT),
        name="attend_forward",
    )(x, positions, w_qkv, ids[:, None, :], ids[:, :, None])


def middle_kernel(
    x_ref,
    pos_ref,
    mixed_ref,
    cot_ref,
    w_out,
    w_up,
    w_down,
    norm_ref,
    result_ref,
    mid_ref,
    gmixed_ref,
    dout_ref,
    dup_ref,
    ddown_ref,
    dnorm_ref,
    act,
    slope,
    gpre,
    acc_out,
    acc_up,
    acc_down,
):
    step = pl.program_id(0)
    last = pl.num_programs(0) - 1
    win, width = pos_ref.shape
    tile = w_up.shape[2]
    ups = w_up.shape[0]
    blocks = w_down.shape[0] // 2

    @pl.when(step == 0)
    def _():
        acc_out[...] = jnp.zeros_like(acc_out)
        acc_up[...] = jnp.zeros_like(acc_up)
        acc_down[...] = jnp.zeros_like(acc_down)
        dnorm_ref[...] = jnp.zeros_like(dnorm_ref)

    mixed = mixed_ref[0]
    hidden = x_ref[...].reshape(win, width).astype(F32) + pos_ref[...]
    attn = jnp.concatenate([nn(mixed, w_out[t]) for t in range(w_out.shape[0])], axis=1)
    scaled_one, inverse_one = row_norm(hidden + attn)
    normed = scaled_one * norm_ref[0:1] + norm_ref[1:2]
    low = normed.astype(BF)
    for t in range(ups):
        pre = nn(low, w_up[t])
        square = pre * pre
        bent = jnp.tanh(GELU_A * pre * (1.0 + GELU_B * square))
        act[:, t * tile : (t + 1) * tile] = (0.5 * pre * (1.0 + bent)).astype(BF)
        slope[:, t * tile : (t + 1) * tile] = (
            0.5 * (1.0 + bent)
            + 0.5 * pre * (1.0 - bent * bent) * (GELU_A + 3.0 * GELU_A * GELU_B * square)
        ).astype(BF)
    branch = jnp.concatenate(
        [
            sum(nn(act[:, b * width : (b + 1) * width], w_down[2 * b + j]) for b in range(blocks))
            for j in range(2)
        ],
        axis=1,
    )
    scaled_two, inverse_two = row_norm(normed + branch)
    result = scaled_two * norm_ref[2:3] + norm_ref[3:4]
    result_ref[...] = result.astype(BF).reshape(result_ref.shape)
    grad_resid, gain_two, shift_two = norm_pull(
        cot_ref[...].reshape(win, width).astype(F32), scaled_two, inverse_two, norm_ref[2:3]
    )
    gb = grad_resid.astype(BF)
    for b in range(blocks):
        cols = slice(b * width, (b + 1) * width)
        gact = nt(gb[:, :tile], w_down[2 * b]) + nt(gb[:, tile:], w_down[2 * b + 1])
        gpre[:, cols] = (gact * slope[:, cols].astype(F32)).astype(BF)
    grad_normed = grad_resid + sum(
        nt(gpre[:, t * tile : (t + 1) * tile], w_up[t]) for t in range(ups)
    )
    grad_mid, gain_one, shift_one = norm_pull(grad_normed, scaled_one, inverse_one, norm_ref[0:1])
    mid_ref[0] = grad_mid
    ga = grad_mid.astype(BF)
    gmixed_ref[0] = sum(
        nt(ga[:, t * tile : (t + 1) * tile], w_out[t]) for t in range(w_out.shape[0])
    ).astype(BF)
    dnorm_ref[...] += jnp.concatenate([gain_one, shift_one, gain_two, shift_two], axis=0)
    for b in range(blocks):
        act_t = act[:, b * width : (b + 1) * width].T
        for j in range(2):
            acc_down[2 * b + j] += nn(act_t, gb[:, j * tile : (j + 1) * tile])
    low_t = low.T
    for t in range(ups):
        acc_up[t] += nn(low_t, gpre[:, t * tile : (t + 1) * tile])
    mixed_t = mixed.T
    for t in range(w_out.shape[0]):
        acc_out[t] += nn(mixed_t, ga[:, t * tile : (t + 1) * tile])

    @pl.when(step == last)
    def _():
        dout_ref[...] = acc_out[...].astype(BF)
        dup_ref[...] = acc_up[...].astype(BF)
        ddown_ref[...] = acc_down[...].astype(BF)


def middle(x, positions, mixed, cot, w_out, w_up, w_down, norms):
    group, wins, span, width = x.shape
    win = group * span
    hidden = w_up.shape[0] * w_up.shape[2]

    def whole(shape):
        return pl.BlockSpec(shape, lambda i: (0,) * len(shape))

    seq_spec = pl.BlockSpec((group, 1, span, width), lambda i: (0, i, 0, 0))
    row_spec = pl.BlockSpec((1, win, width), lambda i: (i, 0, 0))
    return pl.pallas_call(
        middle_kernel,
        grid=(wins,),
        in_specs=[
            seq_spec,
            whole((win, width)),
            row_spec,
            seq_spec,
            whole(w_out.shape),
            whole(w_up.shape),
            whole(w_down.shape),
            whole(norms.shape),
        ],
        out_specs=[
            seq_spec,
            row_spec,
            row_spec,
            whole(w_out.shape),
            whole(w_up.shape),
            whole(w_down.shape),
            whole(norms.shape),
        ],
        out_shape=[
            jax.ShapeDtypeStruct(x.shape, BF),
            jax.ShapeDtypeStruct((wins, win, width), F32),
            jax.ShapeDtypeStruct((wins, win, width), BF),
            jax.ShapeDtypeStruct(w_out.shape, BF),
            jax.ShapeDtypeStruct(w_up.shape, BF),
            jax.ShapeDtypeStruct(w_down.shape, BF),
            jax.ShapeDtypeStruct(norms.shape, F32),
        ],
        scratch_shapes=[
            pltpu.VMEM((win, hidden), BF),
            pltpu.VMEM((win, hidden), BF),
            pltpu.VMEM((win, hidden), BF),
            pltpu.VMEM(w_out.shape, F32),
            pltpu.VMEM(w_up.shape, F32),
            pltpu.VMEM(w_down.shape, F32),
        ],
        compiler_params=pltpu.CompilerParams(vmem_limit_bytes=VMEM_LIMIT),
        name="middle",
    )(x, positions, mixed, cot, w_out, w_up, w_down, norms)


def attend_back_kernel(
    x_ref,
    pos_ref,
    qkv_ref,
    lse_ref,
    gmixed_ref,
    mid_ref,
    w_ref,
    ids_row,
    ids_col,
    dqkv_ref,
    ginput_ref,
    bias,
    gproj,
    acc,
):
    step = pl.program_id(0)
    last = pl.num_programs(0) - 1
    win, width = pos_ref.shape
    dim = width // H
    tile = w_ref.shape[2]
    factor = dim**-0.5
    half = win // 2

    @pl.when(step == 0)
    def _():
        acc[...] = jnp.zeros_like(acc)

    key = lax.broadcasted_iota(jnp.int32, (win, win), 0)
    query_at = lax.broadcasted_iota(jnp.int32, (win, win), 1)
    allowed = (ids_col[0] == ids_row[0]) & (query_at >= key)
    bias[...] = jnp.where(allowed, 0.0, MASKED)
    for pair in range(H // 2):
        packed = []
        for h in (2 * pair, 2 * pair + 1):
            base = 3 * dim * h
            query = qkv_ref[0, :, base : base + dim] * factor
            keys = qkv_ref[0, :, base + dim : base + 2 * dim]
            values = qkv_ref[0, :, base + 2 * dim : base + 3 * dim]
            gout = gmixed_ref[0, :, h * dim : (h + 1) * dim]
            lse = lse_ref[0, h : h + 1, :]
            blocks = []
            inner_late = None
            for lo, first in ((half, half), (0, 0)):
                scores = nt(keys[lo : lo + half], query[first:]) + bias[lo : lo + half, first:]
                probs = jnp.exp(scores - lse[:, first:])
                gprobs = nt(values[lo : lo + half], gout[first:])
                inner = jnp.sum(probs * gprobs, axis=0, keepdims=True)
                blocks.append((probs, gprobs, inner))
            (probs_b, gprobs_b, inner_b), (probs_a, gprobs_a, inner_a) = blocks
            inner_late = inner_a[:, half:] + inner_b
            inner_full = jnp.concatenate([inner_a[:, :half], inner_late], axis=1)
            gs_a = (probs_a * (gprobs_a - inner_full)).astype(BF)
            gs_b = (probs_b * (gprobs_b - inner_late)).astype(BF)
            gvalues = jnp.concatenate(
                [nn(probs_a.astype(BF), gout), nn(probs_b.astype(BF), gout[half:])], axis=0
            )
            gkeys = jnp.concatenate([nn(gs_a, query), nn(gs_b, query[half:])], axis=0)
            gq_a = tn(gs_a, keys[:half])
            gq_b = tn(gs_b, keys[half:])
            gquery = jnp.concatenate([gq_a[:half], gq_a[half:] + gq_b], axis=0) * factor
            packed += [gquery.astype(BF), gkeys.astype(BF), gvalues.astype(BF)]
        gproj[:, pair * 6 * dim : (pair + 1) * 6 * dim] = jnp.concatenate(packed, axis=1)
    hidden = x_ref[...].reshape(win, width).astype(F32) + pos_ref[...]
    low_t = hidden.astype(BF).T
    total = mid_ref[0]
    for t in range(w_ref.shape[0]):
        part = gproj[:, t * tile : (t + 1) * tile]
        acc[t] += nn(low_t, part)
        total += nt(part, w_ref[t])
    ginput_ref[...] = total.astype(BF).reshape(ginput_ref.shape)

    @pl.when(step == last)
    def _():
        dqkv_ref[...] = acc[...].astype(BF)


def attend_backward(x, positions, qkv, lse, gmixed, mid, w_qkv, ids):
    group, wins, span, width = x.shape
    win = group * span
    seq_spec = pl.BlockSpec((group, 1, span, width), lambda i: (0, i, 0, 0))
    return pl.pallas_call(
        attend_back_kernel,
        grid=(wins,),
        in_specs=[
            seq_spec,
            pl.BlockSpec((win, width), lambda i: (0, 0)),
            pl.BlockSpec((1, win, 3 * width), lambda i: (i, 0, 0)),
            pl.BlockSpec((1, H, win), lambda i: (i, 0, 0)),
            pl.BlockSpec((1, win, width), lambda i: (i, 0, 0)),
            pl.BlockSpec((1, win, width), lambda i: (i, 0, 0)),
            pl.BlockSpec(w_qkv.shape, lambda i: (0, 0, 0)),
            pl.BlockSpec((1, 1, win), lambda i: (i, 0, 0)),
            pl.BlockSpec((1, win, 1), lambda i: (i, 0, 0)),
        ],
        out_specs=[pl.BlockSpec(w_qkv.shape, lambda i: (0, 0, 0)), seq_spec],
        out_shape=[
            jax.ShapeDtypeStruct(w_qkv.shape, BF),
            jax.ShapeDtypeStruct(x.shape, BF),
        ],
        scratch_shapes=[
            pltpu.VMEM((win, win), F32),
            pltpu.VMEM((win, 3 * width), BF),
            pltpu.VMEM(w_qkv.shape, F32),
        ],
        compiler_params=pltpu.CompilerParams(vmem_limit_bytes=VMEM_LIMIT),
        name="attend_backward",
    )(x, positions, qkv, lse, gmixed, mid, w_qkv, ids[:, None, :], ids[:, :, None])


def swap(x, axis, bit):
    size = lax.axis_size(axis)
    return lax.ppermute(x, axis, [(i, i ^ bit) for i in range(size)])


def groups_of(axis, group):
    size = lax.axis_size(axis)
    if group == size:
        return None
    return [[base + i for i in range(group)] for base in range(0, size, group)]


def exchange(x, axis, group):
    return lax.all_to_all(
        x, axis, 0, 0, axis_index_groups=groups_of(axis, group), tiled=True
    )


def spread(x, axis):
    size = lax.axis_size(axis)
    return lax.all_to_all(jnp.broadcast_to(x[None], (size,) + x.shape), axis, 0, 0, tiled=True)


def pick(x, index, axis):
    return lax.dynamic_index_in_dim(x, index, axis, keepdims=False)


def in_order(second, own, other, axis):
    low = jnp.where(second == 0, own, other)
    high = jnp.where(second == 0, other, own)
    return jnp.stack([low, high], axis=axis)


def body(
    inputs,
    cotangent,
    segments,
    owners,
    weights,
    left_bases,
    right_bases,
    moment_one,
    moment_two,
    norm_params,
    norm_one,
    norm_two,
    positions,
    pos_one,
    pos_two,
):
    seqs = lax.axis_size("seq")
    reps = lax.axis_size("rep")
    me_s = lax.axis_index("seq")
    me_r = lax.axis_index("rep")
    core = me_r & 1
    seq_local, span, width = inputs.shape
    rows_dev, slots, tile = weights.shape
    tiles = owners.shape[0]
    half = rows_dev // 2
    group = WIN // span
    place = me_s % group
    wins = seq_local // group

    x = exchange(inputs, "seq", group).reshape(group, wins, span, width)
    cot = exchange(cotangent, "seq", group).reshape(group, wins, span, width)
    ids = segments[None]
    bit = 1
    while bit < group:
        ids = jnp.concatenate([ids, swap(ids, "seq", bit)], axis=0)
        bit *= 2
    ids = jnp.take(ids, jnp.arange(group) ^ place, axis=0)
    ids = lax.dynamic_slice_in_dim(ids, place * wins, wins, 1)
    ids = ids.transpose(1, 0, 2).reshape(wins, WIN)

    low_w = weights.astype(BF).transpose(1, 0, 2)
    kept = lax.dynamic_slice_in_dim(low_w, core * half, half, 1)
    sent = lax.dynamic_slice_in_dim(low_w, (1 - core) * half, half, 1)
    buf = jnp.concatenate([kept, swap(sent, "rep", 1)], axis=0)
    bit = 2
    while bit < reps:
        buf = jnp.concatenate([buf, swap(buf, "rep", bit)], axis=0)
        bit *= 2
    by_tile = jnp.take(buf, ((owners // slots) ^ me_r) * slots + owners % slots, axis=0)

    def gather_tiles(some):
        count = some.shape[0]
        rows = spread(some, "seq")
        both = in_order(core, rows, swap(rows, "rep", 1), 1)
        return both.transpose(2, 0, 1, 3, 4).reshape(count, rows_dev * seqs, tile)

    qkv_tiles = 3 * width // tile
    out_tiles = width // tile
    up_tiles = (tiles - qkv_tiles - out_tiles) // 2
    w_qkv = gather_tiles(by_tile[:qkv_tiles])
    w_rest = gather_tiles(by_tile[qkv_tiles:])
    w_out = w_rest[:out_tiles]
    w_up = w_rest[out_tiles : out_tiles + up_tiles]
    w_down = w_rest[out_tiles + up_tiles :]

    qkv, mixed, lse = attend_forward(x, positions, w_qkv, ids)
    result, mid, gmixed, d_out, d_up, d_down, d_norm = middle(
        x, positions, mixed, cot, w_out, w_up, w_down, norm_params
    )
    result = exchange(result.reshape(seq_local, span, width), "seq", group)

    def reduce_tiles(grads):
        count = grads.shape[0]
        parts = grads.reshape(count, seqs, 2, half, tile)
        own = pick(parts, core, 2).astype(F32)
        got = swap(pick(parts, 1 - core, 2), "rep", 1).astype(F32)
        mine = (own + got).astype(BF).transpose(1, 0, 2, 3)
        came = lax.all_to_all(mine, "seq", 0, 0, tiled=True)
        return jnp.sum(came.astype(F32), axis=0).astype(BF)

    g_rest = reduce_tiles(jnp.concatenate([d_out, d_up, d_down], axis=0))
    d_qkv, g_input = attend_backward(x, positions, qkv, lse, gmixed, mid, w_qkv, ids)
    g_qkv = reduce_tiles(d_qkv)
    g_input = exchange(g_input.reshape(seq_local, span, width), "seq", group).astype(F32)

    g_tiles = jnp.concatenate([g_qkv, g_rest], axis=0)
    tile_of = jnp.argsort(owners)
    order = ((jnp.arange(reps) ^ me_r)[:, None] * slots + jnp.arange(slots)[None, :]).reshape(-1)
    buf = jnp.take(g_tiles, jnp.take(tile_of, order), axis=0)
    bit = reps // 2
    while bit > 1:
        cut = bit * slots
        got = swap(buf[cut:], "rep", bit)
        buf = (buf[:cut].astype(F32) + got.astype(F32)).astype(BF)
        bit //= 2
    rows = in_order(core, buf[:slots], swap(buf[slots:], "rep", 1), 1).reshape(
        slots, rows_dev, tile
    )

    low_right = right_bases.astype(BF)
    low_left = left_bases.astype(BF)
    cols = tile // seqs

    def to_columns(values):
        return values.reshape(slots, rows_dev, seqs, cols).transpose(2, 1, 0, 3)

    def from_columns(values):
        return values.reshape(seqs, rows_dev, slots, cols).transpose(2, 1, 0, 3).reshape(
            slots, rows_dev, tile
        )

    turned = jnp.einsum("src,scd->srd", rows, low_right, preferred_element_type=F32).astype(BF)
    turned = lax.all_to_all(to_columns(turned), "seq", 0, 0, tiled=True)
    turned = turned.reshape(seqs * rows_dev, slots, cols)
    turned = jnp.einsum("sir,isc->rsc", low_left, turned, preferred_element_type=F32)
    moments = jnp.concatenate(
        [
            to_columns(moment_one.astype(BF).transpose(1, 0, 2)),
            to_columns(moment_two.astype(BF).transpose(1, 0, 2)),
        ],
        axis=2,
    )
    moments = lax.all_to_all(moments, "seq", 0, 0, tiled=True).astype(F32)
    moments = moments.reshape(seqs * rows_dev, 2 * slots, cols)
    direction = adam_step(turned, moments[:, :slots], moments[:, slots:])[2]
    change = jnp.einsum("sir,rsc->isc", low_left, direction.astype(BF), preferred_element_type=F32)
    back = jnp.concatenate([change, turned], axis=1).astype(BF)
    back = back.reshape(seqs, rows_dev, 2 * slots, cols)
    back = lax.all_to_all(back, "seq", 0, 0, tiled=True)
    change = from_columns(back[:, :, :slots])
    change = jnp.einsum("src,sdc->rsd", change, low_right, preferred_element_type=F32)
    turned = from_columns(back[:, :, slots:]).transpose(1, 0, 2).astype(F32)
    first_new, second_new, _ = adam_step(turned, moment_one, moment_two)
    new_weights = weights - LEARN * (change + DECAY * weights)

    pos_part = jnp.sum(g_input, axis=0)
    pad = jnp.zeros((8 - d_norm.shape[0], width), F32)
    small = jnp.concatenate([pos_part, d_norm, pad], axis=0)
    bit = 1
    while bit < reps:
        small = small + swap(small, "rep", bit)
        bit *= 2
    bit = group
    while bit < seqs:
        small = small + swap(small, "seq", bit)
        bit *= 2
    small = small[None]
    bit = 1
    while bit < group:
        small = jnp.concatenate([small, swap(small, "seq", bit)], axis=0)
        bit *= 2
    grad_norms = jnp.sum(small[:, span : span + 4], axis=0)
    grad_pos = jnp.take(small[:, :span], jnp.arange(group) ^ place, axis=0).reshape(WIN, width)
    norm_first, norm_second, norm_dir = adam_step(grad_norms, norm_one, norm_two)
    pos_first, pos_second, pos_dir = adam_step(grad_pos, pos_one, pos_two)
    return (
        result,
        g_input,
        first_new,
        second_new,
        new_weights,
        norm_first,
        norm_second,
        norm_params - LEARN_SMALL * norm_dir,
        pos_first,
        pos_second,
        positions - LEARN_SMALL * pos_dir,
    )


def solution(mesh):
    tokens = P("rep", "seq", None)
    slots = P("seq", "rep", None)
    bases = P("rep", None, None)
    return jax.shard_map(
        body,
        mesh=mesh,
        in_specs=(
            tokens,
            tokens,
            P("rep", "seq"),
            P(),
            slots,
            bases,
            bases,
            slots,
            slots,
            P(),
            P(),
            P(),
            P(),
            P(),
            P(),
        ),
        out_specs=(tokens, tokens, slots, slots, slots, P(), P(), P(), P(), P(), P()),
        check_vma=False,
    )
```

time: 965 us -> 457 us (0.47)
  waiting for transfers between devices: 427 us -> 167 us
  matrix products: 124 us -> 8.74 us
  local copies, waits for them, and re-layouts: 161 us -> 45.9 us
  blocking collectives: 154 us -> 57.3 us
  Pallas kernels: 0 us -> 62.1 us
  starting transfers between devices: 21.5 us -> 66 us
  other arithmetic: 57.9 us -> 39.2 us
  between operations: 14.9 us -> 1.85 us
    reduce_scatter x3 -> x0, waiting for transfers between devices: 181 us -> none  [the longest x1 66.2 us: body(): lax.psum_scatter(jnp.einsum('sir,rsd->isd', own_cols, change, precision=H...]
    dot_general x22 -> x4, matrix products: 124 us -> 8.74 us  [the longest x1 3.85 us: body(): jnp.einsum('sir,rsc->isc', low_left, direction.astype(BF), preferred_elem...]
    all_gather x1 -> x0, blocking collectives: 114 us -> none  [body(): all_ids = lax.all_gather(segments, 'seq', axis=1, tiled=True)]
    all_gather x2 -> x0, waiting for transfers between devices: 93.2 us -> none  [the longest x1 48.6 us: body(): lax.all_gather(weights.astype(jnp.bfloat16), 'seq', axis=0, tiled=True)]
    psum x1 -> x0, waiting for transfers between devices: 80.8 us -> none  [body(): grad_norms, grad_pos = lax.psum((grad_norms, grad_pos), ('seq', 'rep'))]
    pallas_call x0 -> x3, Pallas kernels: none -> 62.1 us  [the longest x1 26.9 us: middle(): pl.pallas_call(middle_kernel, grid=(wins,), in_specs=[seq_spec, whole((wi...]
    all_to_all x0 -> x1, blocking collectives: none -> 57.3 us  [spread(): lax.all_to_all(jnp.broadcast_to(x[None], (size,) + x.shape), axis, 0, 0,...]
    all_to_all x4 -> x10, waiting for transfers between devices: 71.6 us -> 128 us  [the longest x2 62.9 us: reduce_tiles(): came = lax.all_to_all(mine, 'seq', 0, 0, tiled=True)]
  transfers between devices with their start and end apart: 10 -> 26, of which waited for: 8 -> 15; matrix products, arithmetic and copies ran while one was open for 9% -> 18% of each run, Pallas kernels for 0% -> 14%
where the time goes in v1:
time: 457 us; the launch traced here: 448 us
  waiting for transfers between devices  167 us (37%)
  starting transfers between devices  66 us (14%)
  Pallas kernels  62.1 us (14%)
  blocking collectives  57.3 us (13%)
  local copies, waits for them, and re-layouts  45.9 us (10%)
  other arithmetic  39.2 us (9%)
  matrix products  8.74 us (2%)
    all_to_all x2, waiting for transfers between devices, reduce_tiles(): came = lax.all_to_all(mine, 'seq', 0, 0, tiled=True)  62.9 us
    all_to_all x1, blocking collectives, spread(): lax.all_to_all(jnp.broadcast_to(x[None], (size,) + x.shape), axis, 0, 0,...  57.3 us
    all_to_all x4, waiting for transfers between devices, exchange(): lax.all_to_all(x, axis, 0, 0, axis_index_groups=groups_of(axis, group), t...  45 us
    ppermute x16, waiting for transfers between devices, swap(): return lax.ppermute(x, axis, [(i, i ^ bit) for i in range(size)])  39.4 us
    pallas_call x1, Pallas kernels, middle(): pl.pallas_call(middle_kernel, grid=(wins,), in_specs=[seq_spec, whole((wi...  26.9 us
    ppermute x16, starting transfers between devices, swap(): return lax.ppermute(x, axis, [(i, i ^ bit) for i in range(size)])  21.7 us
    all_to_all x1, waiting for transfers between devices, spread(): lax.all_to_all(jnp.broadcast_to(x[None], (size,) + x.shape), axis, 0, 0,...  19.7 us
    pallas_call x1, Pallas kernels, attend_backward(): pl.pallas_call(attend_back_kernel, grid=(wins,), in_specs=[seq_spec, pl.B...  18.5 us
  transfers between devices with their start and end apart: 26, of which 15 were waited for; matrix products, arithmetic and copies ran while one was open for 18% of the time, Pallas kernels for 14%

profile of v1, /device:TPU:0, one launch (start us, length us, event | category | flops | bytes accessed | tf_op | source)
XLA Modules:
  0.0 448.1 jit_solution(14216199332818286886)
XLA Ops:
  6.8 4.5 %collective-permute-done.1 = bf16[12,32,256]{2,1,0:T(8,128)(2,1)S(1)} collective-permute-done((bf16[12,32,256]{2,1,0:T(8,128)(2,1)S(1)}, bf16[12,32,256]{2,1,0:T(8,128)(2,1)S(1)}, u32[]{:S(2)}, u32[]{:S(2)}) %collective-permute-start.1) | collective-permute-done | bytes 196640 | tf_op jit(solution)/shard_map/ppermute | solution.py:396
  13.0 6.1 %all-to-all-start.1 = ((bf16[8,6,32,256]{3,2,1,0:T(8,128)(2,1)}), bf16[8,6,32,256]{3,2,1,0:T(8,128)(2,1)S(1)}, u32[]{:S(2)}, u32[]{:S(2)}) async-start(bf16[8,6,32,256]{3,2,1,0:T(8,128)(2,1)} %broadcast_in_dim.58), calls=%async_computation.1 | async-start | bytes 1572864 | tf_op jit(solution)/shard_map/all_to_all | solution.py:414
  19.1 19.7 %all-to-all-done.1 = bf16[8,6,32,256]{3,2,1,0:T(8,128)(2,1)S(1)} async-done(((bf16[8,6,32,256]{3,2,1,0:T(8,128)(2,1)}), bf16[8,6,32,256]{3,2,1,0:T(8,128)(2,1)S(1)}, u32[]{:S(2)}, u32[]{:S(2)}) %all-to-all-start.1) | async-done | bytes 786464 | tf_op jit(solution)/shard_map/all_to_all | solution.py:414
  39.2 57.3 %all_to_all.55 = bf16[8,18,32,256]{3,2,1,0:T(8,128)(2,1)S(1)} all-to-all(bf16[8,18,32,256]{3,2,1,0:T(8,128)(2,1)S(1)} %broadcast_in_dim.62), channel_id=1, replica_groups=mesh['seq'=8,'rep'=4] {'seq'}, dimensions={0} | all-to-all | bytes 4718592 | tf_op jit(solution)/shard_map/all_to_all | solution.py:414
  102.2 23.5 %all-to-all-done = bf16[16,64,512]{2,1,0:T(8,128)(2,1)S(1)} async-done(((bf16[16,64,512]{2,1,0:T(8,128)(2,1)}), bf16[16,64,512]{2,1,0:T(8,128)(2,1)S(1)}, u32[]{:S(2)}, u32[]{:S(2)}) %all-to-all-start) | async-done | bytes 1048608 | tf_op jit(solution)/shard_map/all_to_all | solution.py:407
  125.7 4.2 all-to-all-start.2
  141.3 5.4 %collective-permute-done.4 = s32[2,16,64]{2,1,0:T(8,128)S(1)} collective-permute-done((s32[2,16,64]{2,1,0:T(8,128)S(1)}, s32[2,16,64]{2,1,0:T(8,128)S(1)}, u32[]{:S(2)}, u32[]{:S(2)}) %collective-permute-start.4) | collective-permute-done | bytes 8224 | tf_op jit(solution)/shard_map/ppermute | solution.py:396
  146.7 5.0 %collective-permute-start.5 = (s32[4,16,64]{2,1,0:T(8,128)S(1)}, s32[4,16,64]{2,1,0:T(8,128)S(1)}, u32[]{:S(2)}, u32[]{:S(2)}) collective-permute-start(s32[4,16,64]{2,1,0:T(8,128)S(1)} %pad_add_fusion.1), channel_id=1, source_target_pairs={{0,16},{4,20},{8,24},{12,28},{16,0},{20,4},{24,8},{28,12},{1,17},{... | collective-permute-start | bytes 49160 | tf_op jit(solution)/shard_map/ppermute | solution.py:396
  162.0 16.7 %attend_forward.1 = (bf16[2,512,1536]{2,1,0:T(8,128)(2,1)}, bf16[2,512,512]{2,1,0:T(8,128)(2,1)}, f32[2,8,512]{2,1,0:T(8,128)}) custom-call(bf16[8,2,64,512]{3,2,1,0:T(8,128)(2,1)} %bitcast.131, f32[512,512]{1,0:T(8,128)} %pos_ref.5, bf16[6,512,256]{2,1,0:T(8,128)(2,1)} %bitcast.134, s32[2,1,512]{2,1,0:T(1,128)} %broadcast_in_dim_reshape.8.ids_row, ...), custom_call_target="tpu_custom_call" | custom-call | tf_op jit(solution)/shard_map/attend_forward/pallas_call | solution.py:106
  178.7 4.3 all-to-all-start.6
  191.5 26.9 %middle.1 = (bf16[8,2,64,512]{3,2,1,0:T(8,128)(2,1)}, f32[2,512,512]{2,1,0:T(8,128)}, bf16[2,512,512]{2,1,0:T(8,128)(2,1)}, bf16[2,512,256]{2,1,0:T(8,128)(2,1)}...) custom-call(bf16[8,2,64,512]{3,2,1,0:T(8,128)(2,1)} %bitcast.132, ...), custom_call_target="tpu_custom_call" | custom-call | tf_op jit(solution)/shard_map/middle/pallas_call | solution.py:240
  218.4 18.5 %attend_backward.1 = (bf16[6,512,256]{2,1,0:T(8,128)(2,1)}, bf16[8,2,64,512]{3,2,1,0:T(8,128)(2,1)}) custom-call(bf16[8,2,64,512]{3,2,1,0:T(8,128)(2,1)} %bitcast.133, f32[512,512]{1,0:T(8,128)} %pos_ref.5, bf16[2,512,1536]{2,1,0:T(8,128)(2,1)} %get-tuple-element.27.qkv_ref, f32[2,8,512]{2,1,0:T(8,128)} %get-tuple-element.28.lse_ref, ...), custom_call_target="tpu_custom_call" | custom-call | tf_op jit(solution)/shard_map/attend_backward/pallas_call | solution.py:365
  236.9 6.1 %all-to-all-start.5 = ((bf16[16,64,512]{2,1,0:T(8,128)(2,1)}), bf16[16,64,512]{2,1,0:T(8,128)(2,1)S(1)}, u32[]{:S(2)}, u32[]{:S(2)}) async-start(bf16[16,64,512]{2,1,0:T(8,128)(2,1)} %bitcast.149), calls=%async_computation.5 | async-start | bytes 2097152 | tf_op jit(solution)/shard_map/all_to_all | solution.py:407
  248.0 4.9 %collective-permute-done.7 = bf16[6,8,32,256]{3,2,0,1:T(8,128)(2,1)S(1)} collective-permute-done((bf16[6,8,32,256]{3,2,0,1:T(8,128)(2,1)S(1)}, bf16[6,8,32,256]{3,2,0,1:T(8,128)(2,1)S(1)}, u32[]{:S(2)}, u32[]{:S(2)}) %collective-permute-start.7) | collective-permute-done | bytes 786464 | tf_op jit(solution)/shard_map/ppermute | solution.py:396
  254.0 14.0 %all-to-all-done.5 = bf16[16,64,512]{2,1,0:T(8,128)(2,1)S(1)} async-done(((bf16[16,64,512]{2,1,0:T(8,128)(2,1)}), bf16[16,64,512]{2,1,0:T(8,128)(2,1)S(1)}, u32[]{:S(2)}, u32[]{:S(2)}) %all-to-all-start.5) | async-done | bytes 1048608 | tf_op jit(solution)/shard_map/all_to_all | solution.py:407
  268.0 4.2 all-to-all-start.7
  272.2 4.2 fusion.1
  276.4 15.5 %all-to-all-done.7 = bf16[8,6,32,256]{3,2,1,0:T(8,128)(2,1)} async-done(((bf16[8,6,32,256]{3,2,1,0:T(8,128)(2,1)}), bf16[8,6,32,256]{3,2,1,0:T(8,128)(2,1)}, u32[]{:S(2)}, u32[]{:S(2)}) %all-to-all-start.7) | async-done | bytes 786464 | tf_op jit(solution)/shard_map/all_to_all | solution.py:505
  302.1 47.4 %all-to-all-done.8 = bf16[8,18,32,256]{3,2,1,0:T(8,128)(2,1)S(1)} async-done(((bf16[8,18,32,256]{3,2,1,0:T(8,128)(2,1)}), bf16[8,18,32,256]{3,2,1,0:T(8,128)(2,1)S(1)}, u32[]{:S(2)}, u32[]{:S(2)}) %all-to-all-start.8) | async-done | bytes 2359328 | tf_op jit(solution)/shard_map/all_to_all | solution.py:505
  349.5 4.5 %all-to-all-start.4 = ((bf16[16,64,512]{2,1,0:T(8,128)(2,1)}), bf16[16,64,512]{2,1,0:T(8,128)(2,1)}, u32[]{:S(2)}, u32[]{:S(2)}) async-start(bf16[16,64,512]{2,1,0:T(8,128)(2,1)} %bitcast.148), calls=%async_computation.4 | async-start | bytes 2097152 | tf_op jit(solution)/shard_map/all_to_all | solution.py:407
  372.2 7.5 %all-to-all-done.4 = bf16[16,64,512]{2,1,0:T(8,128)(2,1)} async-done(((bf16[16,64,512]{2,1,0:T(8,128)(2,1)}), bf16[16,64,512]{2,1,0:T(8,128)(2,1)}, u32[]{:S(2)}, u32[]{:S(2)}) %all-to-all-start.4) | async-done | bytes 1048608 | tf_op jit(solution)/shard_map/all_to_all | solution.py:407
  379.7 4.0 all-to-all-start.9
  411.3 16.1 %collective-permute-done.15 = f32[4,72,512]{2,1,0:T(8,128)} collective-permute-done((f32[4,72,512]{2,1,0:T(8,128)}, f32[4,72,512]{2,1,0:T(8,128)}, u32[]{:S(2)}, u32[]{:S(2)}) %collective-permute-start.15) | collective-permute-done | bytes 589856 | tf_op jit(solution)/shard_map/ppermute | solution.py:396
  433.9 4.3 multiply_subtract_fusion
  (194 shorter events, 121.5 us)
Async XLA Ops:
  3.2 8.1 %collective-permute-start.1 = (bf16[12,32,256]{2,1,0:T(8,128)(2,1)S(1)}, bf16[12,32,256]{2,1,0:T(8,128)(2,1)S(1)}, u32[]{:S(2)}, u32[]{:S(2)}) collective-permute-start(bf16[12,32,256]{2,1,0:T(8,128)(2,1)S(1)} %pad_maximum_fusion.10), channel_id=1, source_target_pairs={{0,2},{1,3},{2,0},{3,1},{4,6},{5,7},{6,4},{7,5},{8,10},{9,11},{10,... | collective-permute-start | bytes 589832 | tf_op jit(solution)/shard_map/ppermute | solution.py:396
  13.0 25.8 %all-to-all-start.1 = ((bf16[8,6,32,256]{3,2,1,0:T(8,128)(2,1)}), bf16[8,6,32,256]{3,2,1,0:T(8,128)(2,1)S(1)}, u32[]{:S(2)}, u32[]{:S(2)}) async-start(bf16[8,6,32,256]{3,2,1,0:T(8,128)(2,1)} %broadcast_in_dim.58), calls=%async_computation.1 | async-start | bytes 1572864 | tf_op jit(solution)/shard_map/all_to_all | solution.py:414
  96.5 29.2 %all-to-all-start = ((bf16[16,64,512]{2,1,0:T(8,128)(2,1)}), bf16[16,64,512]{2,1,0:T(8,128)(2,1)S(1)}, u32[]{:S(2)}, u32[]{:S(2)}) async-start(bf16[16,64,512]{2,1,0:T(8,128)(2,1)} %param.17), calls=%async_computation | async-start | bytes 2097152 | tf_op jit(solution)/shard_map/all_to_all | solution.py:407
  100.1 82.9 %collective-permute-start.6 = (bf16[8,18,32,256]{3,2,1,0:T(8,128)(2,1)S(1)}, bf16[8,18,32,256]{3,2,1,0:T(8,128)(2,1)}, u32[]{:S(2)}, u32[]{:S(2)}) collective-permute-start(bf16[8,18,32,256]{3,2,1,0:T(8,128)(2,1)S(1)} %all_to_all.55), channel_id=1, source_target_pairs={{0,1},{1,0},{2,3},{3,2},{4,5},{5,4},{6,7},{7,6},{8,9},{9,8},{10,11... | collective-permute-start | bytes 7077896 | tf_op jit(solution)/shard_map/ppermute | solution.py:396
  100.1 39.2 %collective-permute-start.3 = (s32[1,16,64]{2,1,0:T(8,128)S(1)}, s32[1,16,64]{2,1,0:T(8,128)S(1)}, u32[]{:S(2)}, u32[]{:S(2)}) collective-permute-start(s32[1,16,64]{2,1,0:T(8,128)S(1)} %bitcast.152), channel_id=1, source_target_pairs={{0,4},{4,0},{8,12},{12,8},{16,20},{20,16},{24,28},{28,24},{1,5},{5... | collective-permute-start | bytes 12296 | tf_op jit(solution)/shard_map/ppermute | solution.py:396
  125.7 53.0 %all-to-all-start.2 = ((bf16[16,64,512]{2,1,0:T(8,128)(2,1)}), bf16[16,64,512]{2,1,0:T(8,128)(2,1)}, u32[]{:S(2)}, u32[]{:S(2)}) async-start(bf16[16,64,512]{2,1,0:T(8,128)(2,1)} %param.18), calls=%async_computation.2 | async-start | bytes 2097152 | tf_op jit(solution)/shard_map/all_to_all | solution.py:407
  139.2 20.1 %collective-permute-start.2 = (bf16[8,6,32,256]{3,2,1,0:T(8,128)(2,1)}, bf16[8,6,32,256]{3,2,1,0:T(8,128)(2,1)}, u32[]{:S(2)}, u32[]{:S(2)}) collective-permute-start(bf16[8,6,32,256]{3,2,1,0:T(8,128)(2,1)} %copy-done.4), channel_id=1, source_target_pairs={{0,1},{1,0},{2,3},{3,2},{4,5},{5,4},{6,7},{7,6},{8,9},{9,8},{10,11... | collective-permute-start | bytes 2359304 | tf_op jit(solution)/shard_map/ppermute | solution.py:396
  139.3 7.3 %collective-permute-start.4 = (s32[2,16,64]{2,1,0:T(8,128)S(1)}, s32[2,16,64]{2,1,0:T(8,128)S(1)}, u32[]{:S(2)}, u32[]{:S(2)}) collective-permute-start(s32[2,16,64]{2,1,0:T(8,128)S(1)} %pad_add_fusion.2), channel_id=1, source_target_pairs={{0,8},{4,12},{8,0},{12,4},{16,24},{20,28},{24,16},{28,20},{1,9},{5... | collective-permute-start | bytes 24584 | tf_op jit(solution)/shard_map/ppermute | solution.py:396
  146.7 10.0 %collective-permute-start.5 = (s32[4,16,64]{2,1,0:T(8,128)S(1)}, s32[4,16,64]{2,1,0:T(8,128)S(1)}, u32[]{:S(2)}, u32[]{:S(2)}) collective-permute-start(s32[4,16,64]{2,1,0:T(8,128)S(1)} %pad_add_fusion.1), channel_id=1, source_target_pairs={{0,16},{4,20},{8,24},{12,28},{16,0},{20,4},{24,8},{28,12},{1,17},{... | collective-permute-start | bytes 49160 | tf_op jit(solution)/shard_map/ppermute | solution.py:396
  178.7 58.2 %all-to-all-start.6 = ((bf16[8,2,12288]{2,1,0:T(2,128)(2,1)}), bf16[8,2,12288]{2,1,0:T(2,128)(2,1)}, u32[]{:S(2)}, u32[]{:S(2)}) async-start(bf16[8,2,12288]{2,1,0:T(2,128)(2,1)} %reshape.225), calls=%async_computation.6 | async-start | bytes 786432 | tf_op jit(solution)/shard_map/all_to_all | solution.py:550
  236.9 31.1 %all-to-all-start.5 = ((bf16[16,64,512]{2,1,0:T(8,128)(2,1)}), bf16[16,64,512]{2,1,0:T(8,128)(2,1)S(1)}, u32[]{:S(2)}, u32[]{:S(2)}) async-start(bf16[16,64,512]{2,1,0:T(8,128)(2,1)} %bitcast.149), calls=%async_computation.5 | async-start | bytes 2097152 | tf_op jit(solution)/shard_map/all_to_all | solution.py:407
  247.2 25.0 %collective-permute-start.8 = (bf16[18,8,32,256]{3,2,0,1:T(8,128)(2,1)}, bf16[18,8,32,256]{3,2,0,1:T(8,128)(2,1)}, u32[]{:S(2)}, u32[]{:S(2)}) collective-permute-start(bf16[18,8,32,256]{3,2,0,1:T(8,128)(2,1)} %bitcast.127), channel_id=1, source_target_pairs={{0,1},{1,0},{2,3},{3,2},{4,5},{5,4},{6,7},{7,6},{8,9},{9,8},{10,11... | collective-permute-start | bytes 7077896 | tf_op jit(solution)/shard_map/ppermute | solution.py:396
  268.0 23.9 %all-to-all-start.7 = ((bf16[8,6,32,256]{3,2,1,0:T(8,128)(2,1)}), bf16[8,6,32,256]{3,2,1,0:T(8,128)(2,1)}, u32[]{:S(2)}, u32[]{:S(2)}) async-start(bf16[8,6,32,256]{3,2,1,0:T(8,128)(2,1)} %fusion.21), calls=%async_computation.7 | async-start | bytes 1572864 | tf_op jit(solution)/shard_map/all_to_all | solution.py:505
  291.9 57.5 %all-to-all-start.8 = ((bf16[8,18,32,256]{3,2,1,0:T(8,128)(2,1)}), bf16[8,18,32,256]{3,2,1,0:T(8,128)(2,1)S(1)}, u32[]{:S(2)}, u32[]{:S(2)}) async-start(bf16[8,18,32,256]{3,2,1,0:T(8,128)(2,1)} %fusion.1), calls=%async_computation.8 | async-start | bytes 4718592 | tf_op jit(solution)/shard_map/all_to_all | solution.py:505
  301.5 53.1 %collective-permute-start.11 = (f32[72,512]{1,0:T(8,128)S(1)}, f32[72,512]{1,0:T(8,128)S(1)}, u32[]{:S(2)}, u32[]{:S(2)}) collective-permute-start(f32[72,512]{1,0:T(8,128)S(1)} %maximum_maximum_fusion), channel_id=1, source_target_pairs={{0,1},{1,0},{2,3},{3,2},{4,5},{5,4},{6,7},{7,6},{8,9},{9,8},{10,11... | collective-permute-start | bytes 442376 | tf_op jit(solution)/shard_map/ppermute | solution.py:396
  349.5 30.2 %all-to-all-start.4 = ((bf16[16,64,512]{2,1,0:T(8,128)(2,1)}), bf16[16,64,512]{2,1,0:T(8,128)(2,1)}, u32[]{:S(2)}, u32[]{:S(2)}) async-start(bf16[16,64,512]{2,1,0:T(8,128)(2,1)} %bitcast.148), calls=%async_computation.4 | async-start | bytes 2097152 | tf_op jit(solution)/shard_map/all_to_all | solution.py:407
  354.7 5.2 %collective-permute-start.12 = (f32[72,512]{1,0:T(8,128)S(1)}, f32[72,512]{1,0:T(8,128)S(1)}, u32[]{:S(2)}, u32[]{:S(2)}) collective-permute-start(f32[72,512]{1,0:T(8,128)S(1)} %fusion.43), channel_id=1, source_target_pairs={{0,2},{1,3},{2,0},{3,1},{4,6},{5,7},{6,4},{7,5},{8,10},{9,11},{10,... | collective-permute-start | bytes 442376 | tf_op jit(solution)/shard_map/ppermute | solution.py:396
  359.0 5.8 %collective-permute-start.9 = (bf16[12,32,256]{2,1,0:T(8,128)(2,1)S(1)}, bf16[12,32,256]{2,1,0:T(8,128)(2,1)S(1)}, u32[]{:S(2)}, u32[]{:S(2)}) collective-permute-start(bf16[12,32,256]{2,1,0:T(8,128)(2,1)S(1)} %slice.89), channel_id=1, source_target_pairs={{0,2},{1,3},{2,0},{3,1},{4,6},{5,7},{6,4},{7,5},{8,10},{9,11},{10,... | collective-permute-start | bytes 589832 | tf_op jit(solution)/shard_map/ppermute | solution.py:396
  360.8 7.2 %collective-permute-start.13 = (f32[1,72,512]{2,1,0:T(8,128)S(1)}, f32[1,72,512]{2,1,0:T(8,128)S(1)}, u32[]{:S(2)}, u32[]{:S(2)}) collective-permute-start(f32[1,72,512]{2,1,0:T(8,128)S(1)} %add_bitcast_fusion), channel_id=1, source_target_pairs={{0,4},{4,0},{8,12},{12,8},{16,20},{20,16},{24,28},{28,24},{1,5},{5... | collective-permute-start | bytes 442376 | tf_op jit(solution)/shard_map/ppermute | solution.py:396
  364.9 5.7 %collective-permute-start.10 = (bf16[6,32,256]{2,1,0:T(8,128)(2,1)S(1)}, bf16[6,32,256]{2,1,0:T(8,128)(2,1)S(1)}, u32[]{:S(2)}, u32[]{:S(2)}) collective-permute-start(bf16[6,32,256]{2,1,0:T(8,128)(2,1)S(1)} %slice.91), channel_id=1, source_target_pairs={{0,1},{1,0},{2,3},{3,2},{4,5},{5,4},{6,7},{7,6},{8,9},{9,8},{10,11... | collective-permute-start | bytes 294920 | tf_op jit(solution)/shard_map/ppermute | solution.py:396
  368.8 23.0 %collective-permute-start.14 = (f32[2,72,512]{2,1,0:T(8,128)}, f32[2,72,512]{2,1,0:T(8,128)}, u32[]{:S(2)}, u32[]{:S(2)}) collective-permute-start(f32[2,72,512]{2,1,0:T(8,128)} %pad_maximum_fusion.9), channel_id=1, source_target_pairs={{0,8},{4,12},{8,0},{12,4},{16,24},{20,28},{24,16},{28,20},{1,9},{5... | collective-permute-start | bytes 884744 | tf_op jit(solution)/shard_map/ppermute | solution.py:396
  379.7 16.7 %all-to-all-start.9 = ((bf16[8,2,6144]{2,1,0:T(2,128)(2,1)}), bf16[8,2,6144]{2,1,0:T(2,128)(2,1)}, u32[]{:S(2)}, u32[]{:S(2)}) async-start(bf16[8,2,6144]{2,1,0:T(2,128)(2,1)} %reshape.227), calls=%async_computation.9 | async-start | bytes 393216 | tf_op jit(solution)/shard_map/all_to_all | solution.py:540
  393.6 33.8 %collective-permute-start.15 = (f32[4,72,512]{2,1,0:T(8,128)}, f32[4,72,512]{2,1,0:T(8,128)}, u32[]{:S(2)}, u32[]{:S(2)}) collective-permute-start(f32[4,72,512]{2,1,0:T(8,128)} %pad_maximum_fusion.6), channel_id=1, source_target_pairs={{0,16},{4,20},{8,24},{12,28},{16,0},{20,4},{24,8},{28,12},{1,17},{... | collective-permute-start | bytes 1769480 | tf_op jit(solution)/shard_map/ppermute | solution.py:396
  407.6 30.5 %all-to-all-start.10 = ((bf16[8,2,12288]{2,1,0:T(2,128)(2,1)}), bf16[8,2,12288]{2,1,0:T(2,128)(2,1)S(1)}, u32[]{:S(2)}, u32[]{:S(2)}) async-start(bf16[8,2,12288]{2,1,0:T(2,128)(2,1)} %reshape.229), calls=%async_computation.10 | async-start | bytes 786432 | tf_op jit(solution)/shard_map/all_to_all | solution.py:556
  (28 other events, 368.9 us)

commit v2 on v1

v2 whole, which is shorter than its diff:
```python
import functools

import jax
import jax.numpy as jnp
import numpy as np
from jax import lax
from jax.experimental import pallas as pl
from jax.experimental.pallas import tpu as pltpu
from jax.sharding import PartitionSpec as P

H = 8
WIN = 512
STEP = 10

EPS_NORM = 1e-05
EPS_ADAM = 1e-08
BETA = 0.5
LEARN = 0.02
LEARN_SMALL = 0.2
DECAY = 0.01
MASKED = -1e30

BF = jnp.bfloat16
F32 = jnp.float32
PARAMS = pltpu.CompilerParams(vmem_limit_bytes=58 * 1024 * 1024)
GELU_A = 0.7978845608028654
GELU_B = 0.044715


def nn(a, b):
    return lax.dot_general(a, b, (((1,), (0,)), ((), ())), preferred_element_type=F32)


def nt(a, b):
    return lax.dot_general(a, b, (((1,), (1,)), ((), ())), preferred_element_type=F32)


def tn(a, b):
    return lax.dot_general(a, b, (((0,), (0,)), ((), ())), preferred_element_type=F32)


def adam_step(gradient, first, second):
    first_new = BETA * first + (1.0 - BETA) * gradient
    second_new = BETA * second + (1.0 - BETA) * gradient * gradient
    fix = 1.0 - BETA**STEP
    direction = first_new / fix / (jnp.sqrt(second_new / fix) + EPS_ADAM)
    return (first_new, second_new, direction)


def row_norm(values):
    center = values - jnp.mean(values, axis=-1, keepdims=True)
    inverse = lax.rsqrt(jnp.mean(center * center, axis=-1, keepdims=True) + EPS_NORM)
    return center * inverse, inverse


def norm_pull(grad_rows, scaled, inverse, gain):
    scaled_grad = grad_rows * gain
    grad_input = inverse * (
        scaled_grad
        - jnp.mean(scaled_grad, axis=-1, keepdims=True)
        - scaled * jnp.mean(scaled_grad * scaled, axis=-1, keepdims=True)
    )
    grad_gain = jnp.sum(grad_rows * scaled, axis=0, keepdims=True)
    grad_shift = jnp.sum(grad_rows, axis=0, keepdims=True)
    return grad_input, grad_gain, grad_shift


def same(shape):
    return pl.BlockSpec(shape, lambda *_: (0,) * len(shape), pipeline_mode=pl.Buffered(1))


def whole(shape):
    return pl.BlockSpec(shape, lambda *_: (0,) * len(shape))


SCALARS = pl.BlockSpec(memory_space=pltpu.SMEM)


def takes(microseconds):
    return pl.CostEstimate(flops=int(microseconds * 1.1e9), bytes_accessed=0, transcendentals=0)


def gather_masks(order):
    masks = [(0, 0)]
    for axis, bit in order:
        step = (bit, 0) if axis == "seq" else (0, bit)
        masks = masks + [(s ^ step[0], t ^ step[1]) for s, t in masks]
    return tuple(masks)


def beyond(masks):
    return tuple((s, t ^ 1) for s, t in masks)


def block_at(me_ref, mask, reps, rows):
    block = (me_ref[0] ^ mask[0]) * reps + (me_ref[1] ^ mask[1])
    return pl.ds(pl.multiple_of(block * rows, rows), rows)


def place_blocks(me_ref, refs, target, plans, reps):
    if plans is None:
        target[...] = refs[0][...]
        return
    for ref, (first, last, masks) in zip(refs, plans):
        for k, mask in enumerate(masks):
            where = block_at(me_ref, mask, reps, ref.shape[2])
            target[first:last, where, :] = ref[k, : last - first]


def take_blocks(me_ref, source, outs, plans, reps, rows):
    if plans is None:
        outs[0][...] = source[...].astype(BF)
        return
    for out, parts in zip(outs, plans):
        at = 0
        for first, last, masks in parts:
            for mask in masks:
                where = block_at(me_ref, mask, reps, rows)
                out[at : at + last - first] = source[first:last, where, :].astype(BF)
                at += last - first


def attend_kernel(plans, reps, me_ref, x_ref, pos_ref, ids_row, ids_col, *refs):
    count = 1 if plans is None else len(plans)
    pieces = refs[:count]
    qkv_ref, mixed_ref, lse_ref, bias, w_ref = refs[count:]
    win, width = pos_ref.shape
    dim = width // H
    tile = w_ref.shape[2]

    place_blocks(me_ref, pieces, w_ref, plans, reps)
    hidden = x_ref[...].reshape(win, width).astype(F32) + pos_ref[...]
    low = hidden.astype(BF)
    for t in range(w_ref.shape[0]):
        qkv_ref[0, :, t * tile : (t + 1) * tile] = nn(low, w_ref[t]).astype(BF)
    row = lax.broadcasted_iota(jnp.int32, (win, win), 0)
    col = lax.broadcasted_iota(jnp.int32, (win, win), 1)
    allowed = (ids_col[0] == ids_row[0]) & (row >= col)
    bias[...] = jnp.where(allowed, 0.0, MASKED)
    half = win // 2
    sums = []
    for pair in range(H // 2):
        outs = []
        for h in (2 * pair, 2 * pair + 1):
            base = 3 * dim * h
            query = qkv_ref[0, :, base : base + dim] * (dim**-0.5)
            keys = qkv_ref[0, :, base + dim : base + 2 * dim]
            values = qkv_ref[0, :, base + 2 * dim : base + 3 * dim]
            parts, logs = [], []
            for lo, upto in ((0, half), (half, win)):
                scores = nt(query[lo : lo + half], keys[:upto]) + bias[lo : lo + half, :upto]
                highest = jnp.max(scores, axis=-1, keepdims=True)
                powers = jnp.exp(scores - highest)
                total = jnp.sum(powers, axis=-1, keepdims=True)
                parts.append(nn(powers.astype(BF), values[:upto]) / total)
                logs.append(highest + jnp.log(total))
            outs.append(jnp.concatenate(parts, axis=0))
            sums.append(jnp.concatenate(logs, axis=0))
        mixed_ref[0, :, pair * 2 * dim : (pair + 1) * 2 * dim] = jnp.concatenate(outs, axis=1).astype(BF)
    lanes = jnp.concatenate(sums + [jnp.zeros((win, 128 - H), F32)], axis=1)
    lse_ref[0] = lanes.T[:H]


def attend_forward(window, me, x, positions, ids, w, plans, tiles, tile, reps):
    group, span, width = x.shape
    win = group * span
    return pl.pallas_call(
        functools.partial(attend_kernel, plans, reps),
        grid=(1,),
        in_specs=[
            SCALARS,
            whole((group, span, width)),
            same((win, width)),
            pl.BlockSpec((1, 1, win), lambda i: (window, 0, 0)),
            pl.BlockSpec((1, win, 1), lambda i: (window, 0, 0)),
        ]
        + [same(piece.shape) for piece in w],
        out_specs=[whole((1, win, 3 * width)), whole((1, win, width)), whole((1, H, win))],
        out_shape=[
            jax.ShapeDtypeStruct((1, win, 3 * width), BF),
            jax.ShapeDtypeStruct((1, win, width), BF),
            jax.ShapeDtypeStruct((1, H, win), F32),
        ],
        scratch_shapes=[pltpu.VMEM((win, win), F32), pltpu.VMEM((tiles, width, tile), BF)],
        compiler_params=PARAMS,
        cost_estimate=takes(8),
        name="attend_forward",
    )(me, x, positions, ids[:, None, :], ids[:, :, None], *w)


def middle_kernel(
    plans, out_plans, reps, rows, outs, wins, me_ref, pos_ref, cot_ref, norm_ref, moments_ref, *refs
):
    x_refs = refs[:wins]
    mixed_refs = refs[wins : 2 * wins]
    refs = refs[2 * wins :]
    count = 1 if plans is None else len(plans)
    pieces = refs[:count]
    refs = refs[count:]
    result_ref, mid_ref, gmixed_ref, dnorm_ref = refs[:4]
    count = 1 if out_plans is None else 2
    grads = refs[4 : 4 + count]
    x_ref, mixed_ref, act, slope, gpre, w_ref, acc = refs[4 + count :]
    step = pl.program_id(0)
    last = pl.num_programs(0) - 1
    win, width = pos_ref.shape
    tile = w_ref.shape[2]
    ups = (w_ref.shape[0] - outs) // 2
    blocks = ups // 2
    up, down = outs, outs + ups

    @pl.when(step == 0)
    def _():
        place_blocks(me_ref, pieces, w_ref, plans, reps)
        acc[...] = jnp.zeros_like(acc)
        dnorm_ref[...] = jnp.zeros_like(dnorm_ref)

    for window in range(wins):

        @pl.when(step == window)
        def _():
            mixed_ref[...] = mixed_refs[window][0]
            x_ref[...] = x_refs[window][...].reshape(win, width)
            if window == 0 and result_ref.shape[2] > wins * width:
                result_ref[:, :, wins * width :] = moments_ref[...]

    mixed = mixed_ref[...]
    hidden = x_ref[...].astype(F32) + pos_ref[...]
    attn = jnp.concatenate([nn(mixed, w_ref[t]) for t in range(outs)], axis=1)
    scaled_one, inverse_one = row_norm(hidden + attn)
    normed = scaled_one * norm_ref[0:1] + norm_ref[1:2]
    low = normed.astype(BF)
    for t in range(ups):
        pre = nn(low, w_ref[up + t])
        square = pre * pre
        bent = jnp.tanh(GELU_A * pre * (1.0 + GELU_B * square))
        act[:, t * tile : (t + 1) * tile] = (0.5 * pre * (1.0 + bent)).astype(BF)
        slope[:, t * tile : (t + 1) * tile] = (
            0.5 * (1.0 + bent)
            + 0.5 * pre * (1.0 - bent * bent) * (GELU_A + 3.0 * GELU_A * GELU_B * square)
        ).astype(BF)
    branch = jnp.concatenate(
        [
            sum(nn(act[:, b * width : (b + 1) * width], w_ref[down + 2 * b + j]) for b in range(blocks))
            for j in range(2)
        ],
        axis=1,
    )
    scaled_two, inverse_two = row_norm(normed + branch)
    result = (scaled_two * norm_ref[2:3] + norm_ref[3:4]).astype(BF)
    result = result.reshape(*result_ref.shape[:2], width)
    for window in range(wins):

        @pl.when(step == window)
        def _():
            result_ref[:, :, window * width : (window + 1) * width] = result

    grad_resid, gain_two, shift_two = norm_pull(
        cot_ref[...].reshape(win, width).astype(F32), scaled_two, inverse_two, norm_ref[2:3]
    )
    gb = grad_resid.astype(BF)
    for b in range(blocks):
        cols = slice(b * width, (b + 1) * width)
        gact = nt(gb[:, :tile], w_ref[down + 2 * b]) + nt(gb[:, tile:], w_ref[down + 2 * b + 1])
        gpre[:, cols] = (gact * slope[:, cols].astype(F32)).astype(BF)
    grad_normed = grad_resid + sum(
        nt(gpre[:, t * tile : (t + 1) * tile], w_ref[up + t]) for t in range(ups)
    )
    grad_mid, gain_one, shift_one = norm_pull(grad_normed, scaled_one, inverse_one, norm_ref[0:1])
    mid_ref[0] = grad_mid
    ga = grad_mid.astype(BF)
    gmixed_ref[0] = sum(nt(ga[:, t * tile : (t + 1) * tile], w_ref[t]) for t in range(outs)).astype(BF)
    dnorm_ref[...] += jnp.concatenate([gain_one, shift_one, gain_two, shift_two], axis=0)
    for b in range(blocks):
        act_t = act[:, b * width : (b + 1) * width].T
        for j in range(2):
            acc[down + 2 * b + j] += nn(act_t, gb[:, j * tile : (j + 1) * tile])
    low_t = low.T
    for t in range(ups):
        acc[up + t] += nn(low_t, gpre[:, t * tile : (t + 1) * tile])
    mixed_t = mixed.T
    for t in range(outs):
        acc[t] += nn(mixed_t, ga[:, t * tile : (t + 1) * tile])

    @pl.when(step == last)
    def _():
        take_blocks(me_ref, acc, grads, out_plans, reps, rows)


def middle(me, x, positions, mixed, cot, norms, moments, together, w, plans, out_plans, grad_shapes, tiles, tile, reps, rows):
    group, span, width = x[0].shape
    wins = len(x)
    win = group * span
    outs = width // tile
    hidden = (tiles - outs) // 2 * tile
    sent = (group, span, wins * width + (moments.shape[2] if together else 0))
    seq_spec = pl.BlockSpec((group, 1, span, width), lambda i: (0, i, 0, 0))
    row_spec = pl.BlockSpec((1, win, width), lambda i: (i, 0, 0))
    return pl.pallas_call(
        functools.partial(middle_kernel, plans, out_plans, reps, rows, outs, wins),
        grid=(wins,),
        in_specs=[SCALARS, same((win, width)), seq_spec, same(norms.shape), same(moments.shape)]
        + [same(part.shape) for part in x]
        + [same(part.shape) for part in mixed]
        + [same(piece.shape) for piece in w],
        out_specs=[whole(sent), row_spec, row_spec, whole(norms.shape)]
        + [whole(shape) for shape in grad_shapes],
        out_shape=[
            jax.ShapeDtypeStruct(sent, BF),
            jax.ShapeDtypeStruct((wins, win, width), F32),
            jax.ShapeDtypeStruct((wins, win, width), BF),
            jax.ShapeDtypeStruct(norms.shape, F32),
        ]
        + [jax.ShapeDtypeStruct(shape, BF) for shape in grad_shapes],
        scratch_shapes=[
            pltpu.VMEM((win, width), BF),
            pltpu.VMEM((win, width), BF),
            pltpu.VMEM((win, hidden), BF),
            pltpu.VMEM((win, hidden), BF),
            pltpu.VMEM((win, hidden), BF),
            pltpu.VMEM((tiles, width, tile), BF),
            pltpu.VMEM((tiles, width, tile), F32),
        ],
        compiler_params=PARAMS,
        cost_estimate=takes(27),
        name="middle",
    )(me, positions, cot, norms, moments, *x, *mixed, *w)


def attend_back_kernel(
    plans, out_plans, reps, rows, last, me_ref, x_ref, pos_ref, ids_row, ids_col, qkv_ref, lse_ref, gmixed_ref,
    mid_ref, dnorm_ref, *refs,
):
    count = 1 if plans is None else len(plans)
    pieces = refs[:count]
    refs = refs[count:]
    if last:
        older, xs = refs[: 2 * last], refs[2 * last : 3 * last]
        ginput_ref = refs[3 * last]
        refs = refs[3 * last + 1 :]
        count = 1 if out_plans is None else 2
        grads = refs[:count]
        bias, w_ref, gproj, acc = refs[count:]
    else:
        ginput_ref, gproj, bias, w_ref = refs
    win, width = pos_ref.shape
    dim = width // H
    tiles, _, tile = w_ref.shape
    factor = dim**-0.5
    half = win // 2
    place_blocks(me_ref, pieces, w_ref, plans, reps)

    key = lax.broadcasted_iota(jnp.int32, (win, win), 0)
    query_at = lax.broadcasted_iota(jnp.int32, (win, win), 1)
    allowed = (ids_col[0] == ids_row[0]) & (query_at >= key)
    bias[...] = jnp.where(allowed, 0.0, MASKED)
    for pair in range(H // 2):
        packed = []
        for h in (2 * pair, 2 * pair + 1):
            base = 3 * dim * h
            query = qkv_ref[0, :, base : base + dim] * factor
            keys = qkv_ref[0, :, base + dim : base + 2 * dim]
            values = qkv_ref[0, :, base + 2 * dim : base + 3 * dim]
            gout = gmixed_ref[0, :, h * dim : (h + 1) * dim]
            lse = lse_ref[0, h : h + 1, :]
            parts = []
            for lo, first in ((half, half), (0, 0)):
                scores = nt(keys[lo : lo + half], query[first:]) + bias[lo : lo + half, first:]
                probs = jnp.exp(scores - lse[:, first:])
                gprobs = nt(values[lo : lo + half], gout[first:])
                inner = jnp.sum(probs * gprobs, axis=0, keepdims=True)
                parts.append((probs, gprobs, inner))
            (probs_b, gprobs_b, inner_b), (probs_a, gprobs_a, inner_a) = parts
            inner_late = inner_a[:, half:] + inner_b
            inner_full = jnp.concatenate([inner_a[:, :half], inner_late], axis=1)
            gs_a = (probs_a * (gprobs_a - inner_full)).astype(BF)
            gs_b = (probs_b * (gprobs_b - inner_late)).astype(BF)
            gvalues = jnp.concatenate(
                [nn(probs_a.astype(BF), gout), nn(probs_b.astype(BF), gout[half:])], axis=0
            )
            gkeys = jnp.concatenate([nn(gs_a, query), nn(gs_b, query[half:])], axis=0)
            gq_a = tn(gs_a, keys[:half])
            gq_b = tn(gs_b, keys[half:])
            gquery = jnp.concatenate([gq_a[:half], gq_a[half:] + gq_b], axis=0) * factor
            packed += [gquery.astype(BF), gkeys.astype(BF), gvalues.astype(BF)]
        gproj[:, pair * 6 * dim : (pair + 1) * 6 * dim] = jnp.concatenate(packed, axis=1)
    total = mid_ref[0]
    for t in range(tiles):
        total += nt(gproj[:, t * tile : (t + 1) * tile], w_ref[t])
    ginput_ref[...] = total.astype(BF).reshape(ginput_ref.shape)
    if not last:
        return

    hidden = [ref[...].reshape(win, width).astype(F32) + pos_ref[...] for ref in (*xs, x_ref)]
    low_t = [part.astype(BF).T for part in hidden]
    projs = list(older[:last]) + [gproj]
    for t in range(tiles):
        acc[t] = sum(nn(low, proj[:, t * tile : (t + 1) * tile]) for low, proj in zip(low_t, projs))
    for ref in older[last:]:
        total += ref[...].reshape(win, width).astype(F32)
    for j in range(width // tile):
        acc[tiles + j] = total[:, j * tile : (j + 1) * tile]
    if out_plans is not None:
        small = jnp.concatenate(
            [dnorm_ref[:, j * tile : (j + 1) * tile] for j in range(width // tile)], axis=0
        )
        small = jnp.concatenate([small, jnp.zeros((rows - small.shape[0], tile), F32)], axis=0)
        for b in range(win // rows):
            acc[acc.shape[0] - 1, b * rows : (b + 1) * rows] = small
    else:
        acc[acc.shape[0] - 1] = jnp.zeros((win, tile), F32)
    take_blocks(me_ref, acc, grads, out_plans, reps, rows)


def attend_backward(
    window, me, x, positions, ids, qkv, lse, gmixed, mid, dnorm, w, plans, tiles, tile, reps,
    older=None, out_plans=None, grad_shapes=(), rows=0,
):
    group, span, width = x[window].shape
    win = group * span
    last = len(older) // 2 if older is not None else 0
    row_spec = pl.BlockSpec((1, win, width), lambda i: (window, 0, 0))
    out_specs = [whole((group, span, width))]
    out_shape = [jax.ShapeDtypeStruct((group, span, width), BF)]
    scratch = [pltpu.VMEM((win, win), F32), pltpu.VMEM((tiles, width, tile), BF)]
    more = []
    if last:
        more = list(older) + list(x[:window])
        out_specs += [whole(shape) for shape in grad_shapes]
        out_shape += [jax.ShapeDtypeStruct(shape, BF) for shape in grad_shapes]
        scratch += [
            pltpu.VMEM((win, 3 * width), BF),
            pltpu.VMEM((tiles + width // tile + 1, width, tile), F32),
        ]
    else:
        out_specs.append(whole((win, 3 * width)))
        out_shape.append(jax.ShapeDtypeStruct((win, 3 * width), BF))
    return pl.pallas_call(
        functools.partial(attend_back_kernel, plans, out_plans, reps, rows, last),
        grid=(1,),
        in_specs=[
            SCALARS,
            whole((group, span, width)),
            same((win, width)),
            pl.BlockSpec((1, 1, win), lambda i: (window, 0, 0)),
            pl.BlockSpec((1, win, 1), lambda i: (window, 0, 0)),
            whole((1, win, 3 * width)),
            whole((1, H, win)),
            row_spec,
            row_spec,
            same(dnorm.shape),
        ]
        + [same(piece.shape) for piece in w]
        + [same(part.shape) for part in more],
        out_specs=out_specs,
        out_shape=out_shape,
        scratch_shapes=scratch,
        compiler_params=PARAMS,
        cost_estimate=takes(10),
        name="attend_backward",
    )(me, x[window], positions, ids[:, None, :], ids[:, :, None], qkv, lse, gmixed, mid, dnorm, *w, *more)


def right_kernel(rows_ref, right_ref, out_ref):
    seqs, _, _ = out_ref.shape
    slots, _, tile = rows_ref.shape
    cols = tile // seqs
    for s in range(slots):
        turned = nn(rows_ref[s], right_ref[s]).astype(BF)
        for j in range(seqs):
            out_ref[j, :, s * cols : (s + 1) * cols] = turned[:, j * cols : (j + 1) * cols]


def right_turn(rows, right, seqs):
    slots, rows_dev, tile = rows.shape
    return pl.pallas_call(
        right_kernel,
        out_shape=jax.ShapeDtypeStruct((seqs, rows_dev, slots * tile // seqs), BF),
        compiler_params=PARAMS,
        name="right_turn",
    )(rows, right)


def left_kernel(x_ref, moments_ref, left_ref, left_t_ref, out_ref):
    seqs, rows_dev, wide = x_ref.shape
    slots, width, _ = left_ref.shape
    cols = wide // slots
    x = x_ref[...].reshape(width, wide)
    moments = moments_ref[...].reshape(width, 2 * wide).astype(F32)
    turned = [nn(left_t_ref[s], x[:, s * cols : (s + 1) * cols]) for s in range(slots)]
    turned = jnp.concatenate(turned, axis=1)
    direction = adam_step(turned, moments[:, :wide], moments[:, wide:])[2].astype(BF)
    change = [nn(left_ref[s], direction[:, s * cols : (s + 1) * cols]) for s in range(slots)]
    out = jnp.concatenate(change + [turned], axis=1).astype(BF)
    out_ref[...] = out.reshape(out_ref.shape)


def left_turns(x, moments, left, left_t):
    seqs, rows_dev, wide = x.shape
    return pl.pallas_call(
        left_kernel,
        out_shape=jax.ShapeDtypeStruct((seqs, rows_dev, 2 * wide), BF),
        compiler_params=PARAMS,
        name="left_turns",
    )(x, moments, left, left_t)


def last_kernel(back_ref, right_ref, w_ref, one_ref, two_ref, new_one, new_two, new_w):
    seqs, rows_dev, _ = back_ref.shape
    slots, _, tile = w_ref.shape
    cols = tile // seqs
    for s in range(slots):

        def columns(first):
            return jnp.concatenate(
                [back_ref[j, :, first + s * cols : first + (s + 1) * cols] for j in range(seqs)], axis=1
            )

        change = nt(columns(0), right_ref[s])
        turned = columns(slots * cols).astype(F32)
        new_one[s], new_two[s], _ = adam_step(turned, one_ref[s], two_ref[s])
        old = w_ref[s]
        new_w[s] = old - LEARN * (change + DECAY * old)


def last_turn(back, right, weights, one, two):
    shape = jax.ShapeDtypeStruct(weights.shape, F32)
    return pl.pallas_call(
        last_kernel,
        out_shape=[shape, shape, shape],
        compiler_params=PARAMS,
        name="last_turn",
    )(back, right, weights, one, two)


def columns_kernel(one_ref, two_ref, out_ref):
    seqs = out_ref.shape[0]
    slots, _, tile = one_ref.shape
    cols = tile // seqs
    for first, ref in ((0, one_ref), (slots, two_ref)):
        for s in range(slots):
            values = ref[s].astype(BF)
            for j in range(seqs):
                at = (first + s) * cols
                out_ref[j, :, at : at + cols] = values[:, j * cols : (j + 1) * cols]


def moment_columns(one, two, seqs):
    slots, rows_dev, tile = one.shape
    return pl.pallas_call(
        columns_kernel,
        out_shape=jax.ShapeDtypeStruct((seqs, rows_dev, 2 * slots * tile // seqs), BF),
        compiler_params=PARAMS,
        name="moment_columns",
    )(one, two)


def bases_kernel(left_ref, right_ref, low_left, low_left_t, low_right):
    left = left_ref[0].astype(BF)
    low_left[0] = left
    low_left_t[0] = left.T
    low_right[0] = right_ref[0].astype(BF)


def low_bases(left, right):
    slots, width, _ = left.shape
    tile = right.shape[1]
    big = pl.BlockSpec((1, width, width), lambda i: (i, 0, 0))
    little = pl.BlockSpec((1, tile, tile), lambda i: (i, 0, 0))
    return pl.pallas_call(
        bases_kernel,
        grid=(slots,),
        in_specs=[big, little],
        out_specs=[big, big, little],
        out_shape=[
            jax.ShapeDtypeStruct(left.shape, BF),
            jax.ShapeDtypeStruct(left.shape, BF),
            jax.ShapeDtypeStruct(right.shape, BF),
        ],
        compiler_params=PARAMS,
        name="low_bases",
    )(left, right)


def swap(x, axis, bit):
    size = lax.axis_size(axis)
    return lax.ppermute(x, axis, [(i, i ^ bit) for i in range(size)])


def exchange(x, axis, group):
    size = lax.axis_size(axis)
    groups = None
    if group != size:
        groups = [[base + i for i in range(group)] for base in range(0, size, group)]
    return lax.all_to_all(x, axis, 0, 0, axis_index_groups=groups, tiled=True)


def after(x, *others):
    return lax.optimization_barrier((x,) + others)[0]


def powers(first, size):
    bits = []
    while first < size:
        bits.append(first)
        first *= 2
    return bits


def gather(block, order):
    own = block[None]
    for axis, bit in order[:-1]:
        own = jnp.concatenate([own, swap(own, axis, bit)], axis=0)
    return own, swap(own, *order[-1])


def add(a, b, *others):
    if others:
        b = after(b, *others)
    return (a.astype(F32) + b.astype(F32)).astype(BF)


def double(buf, axis, bit, *others):
    got = swap(buf, axis, bit)
    if others:
        got = after(got, *others)
    return jnp.concatenate([buf, got], axis=0)


def halve(buf, axis, bit, *others):
    cut = buf.shape[0] // 2
    return add(buf[:cut], swap(buf[cut:], axis, bit), *others)


def body(
    inputs,
    cotangent,
    segments,
    owners,
    weights,
    left_bases,
    right_bases,
    moment_one,
    moment_two,
    norm_params,
    norm_one,
    norm_two,
    positions,
    pos_one,
    pos_two,
):
    seqs = lax.axis_size("seq")
    reps = lax.axis_size("rep")
    me_s = lax.axis_index("seq")
    me_r = lax.axis_index("rep")
    me = jnp.stack([me_s, me_r]).astype(jnp.int32)
    seq_local, span, width = inputs.shape
    rows_dev, slots, tile = weights.shape
    tiles = owners.shape[0]
    rows = rows_dev // reps
    group = WIN // span
    place = me_s % group
    wins = seq_local // group
    aligned = rows % 16 == 0
    blocks = seqs * reps
    seq_bits = [("seq", b) for b in powers(1, seqs)[::-1]]
    far_bits = [("rep", b) for b in powers(2, reps)]
    core_bit = [("rep", 1)]

    by_window = inputs.reshape(group, wins, span, width)
    x = [exchange(by_window[:, 0], "seq", group)]

    low_w = weights.astype(BF).transpose(1, 0, 2).reshape(slots, reps, rows, tile).transpose(1, 0, 2, 3)
    near = [lax.dynamic_index_in_dim(low_w, me_r, 0, keepdims=False)]
    for k in range(1, reps):
        near.append(swap(lax.dynamic_index_in_dim(low_w, me_r ^ k, 0, keepdims=False), "rep", k))
    near = jnp.concatenate(near, axis=0)
    near = jnp.take(near, ((owners // slots) ^ me_r) * slots + owners % slots, axis=0)
    ids = segments.reshape(-1)
    id_tiles = -(-2 * ids.shape[0] // (rows * tile))
    ids = jnp.concatenate([ids // 64, ids % 64]).astype(BF)
    ids = jnp.pad(ids, (0, id_tiles * rows * tile - ids.shape[0])).reshape(id_tiles, rows, tile)

    qkv_tiles = 3 * width // tile
    rest_tiles = tiles - qkv_tiles
    qkv_at, rest_at = qkv_tiles // 2, rest_tiles // 2
    split = qkv_at + id_tiles
    by_slot = [values.transpose(1, 0, 2) for values in (weights, moment_one, moment_two)]
    rest = near[qkv_tiles:][None]
    near = jnp.concatenate([near[:qkv_at], ids, near[qkv_at:qkv_tiles]], axis=0)[None]
    moments = moment_columns(after(by_slot[1], near), by_slot[2], seqs)
    for i, step in enumerate(seq_bits[:-1]):
        near = double(near, *step, *([moments] if i == 0 else [x[0]]))
        rest = double(after(rest, moments) if i == 0 else rest, *step, near)
    for w in range(1, wins):
        x.append(exchange(after(by_window[:, w], near), "seq", group))
    cot = exchange(after(cotangent, x[-1]), "seq", group).reshape(group, wins, span, width)

    def table_of(masks):
        table = np.zeros(blocks, np.int32)
        for k, (s, t) in enumerate(masks):
            table[s * reps + t] = k
        return jnp.asarray(table)

    orders = [seq_bits[-1:] + far_bits, far_bits + seq_bits[-1:]]

    def pieces_of(bufs, ranges):
        pieces, plans = [], []
        for buf, order, (first, last) in zip(bufs, orders, ranges):
            masks = gather_masks(seq_bits[:-1] + order)
            pieces += [buf, swap(buf, *core_bit[0])]
            plans += [(first, last, masks), (first, last, beyond(masks))]
        return settle(pieces, plans)

    def settle(pieces, plans):
        if aligned:
            return pieces, plans
        at = jnp.arange(blocks)
        full = []
        for i in range(0, len(pieces), 2):
            count = plans[i][1] - plans[i][0]
            table = table_of(plans[i][2] + plans[i + 1][2])
            both = jnp.concatenate([pieces[i][:, :count], pieces[i + 1][:, :count]], axis=0)
            both = jnp.take(both, table[((at // reps) ^ me_s) * reps + ((at % reps) ^ me_r)], axis=0)
            full.append(both.transpose(1, 0, 2, 3).reshape(count, blocks * rows, tile))
        return [jnp.concatenate(full, axis=0)], None

    bufs = [near[:, :split], near[:, split:]]
    bufs = [double(buf, *order[0]) for buf, order in zip(bufs, orders)]
    ids = bufs[0][:, qkv_at:]
    rest = after(rest, *bufs)
    for i in range(1, len(orders[0])):
        bufs = [double(buf, *order[i]) for buf, order in zip(bufs, orders)]
    w_qkv, qkv_plans = pieces_of(bufs, [(0, qkv_at), (qkv_at, qkv_tiles)])
    rest = [rest[:, :rest_at], rest[:, rest_at:]]
    rest = [double(buf, *order[0], *bufs) for buf, order in zip(rest, orders)]

    ids = ids.reshape(seqs, -1)[:, : 2 * seq_local * span].astype(jnp.int32)
    ids = (ids[:, : seq_local * span] * 64 + ids[:, seq_local * span :]).reshape(seqs, seq_local, span)
    spots = [0] * seqs
    for k, (s, _) in enumerate(gather_masks(seq_bits[:-1] + seq_bits[-1:])):
        spots[s] = k
    ids = jnp.take(ids, jnp.asarray(spots[:group])[jnp.arange(group) ^ place], axis=0)
    ids = lax.dynamic_slice_in_dim(ids, place * wins, wins, 1)
    ids = ids.transpose(1, 0, 2).reshape(wins, WIN)

    def scatter_plans(parts):
        count = parts[-1][1]
        if not aligned:
            return None, [(count, blocks * rows, tile)]
        own = [(first, last, gather_masks(order[:0:-1])) for first, last, order in parts]
        other = [(first, last, beyond(masks)) for first, last, masks in own]
        shape = (count * blocks // 2, rows, tile)
        return [own, other], [shape, shape]

    def scatter_tiles(grads, parts, *others):
        if not aligned:
            plain = grads[0].reshape(-1, blocks, rows, tile).transpose(1, 0, 2, 3)
            own, other = [], []
            for first, last, order in parts:
                masks = gather_masks(order[:0:-1])
                for target, some in ((own, masks), (other, beyond(masks))):
                    spots = np.array([s * reps + t for s, t in some])
                    at = ((spots // reps) ^ me_s) * reps + ((spots % reps) ^ me_r)
                    target.append(jnp.take(plain[:, first:last], at, axis=0).reshape(-1, rows, tile))
            grads = [jnp.concatenate(own, axis=0), jnp.concatenate(other, axis=0)]
        return add(grads[0], swap(grads[1], *core_bit[0]), *others)

    def cut_parts(buf, parts):
        out, at = [], 0
        for first, last, _ in parts:
            size = (last - first) * blocks // 2
            out.append(buf[at : at + size])
            at += size
        return out

    def join(bufs, parts):
        entries = 2 ** len(seq_bits[:-1])
        return jnp.concatenate([buf.reshape(entries, -1, rows, tile) for buf in bufs], axis=1)

    zyxc = seq_bits + far_bits + core_bit
    zxyc = seq_bits[:-1] + far_bits + seq_bits[-1:] + core_bit
    ahead = []
    ids = after(ids, *rest)
    for w in range(wins):
        ahead.append(attend_forward(w, me, x[w], positions, ids, w_qkv, qkv_plans, qkv_tiles, tile, reps))
        if w == 0:
            for i in range(1, len(orders[0])):
                rest = [double(buf, *order[i], ahead[0][1]) for buf, order in zip(rest, orders)]
            ids = after(ids, *rest)
    w_rest, rest_plans = pieces_of(rest, [(0, rest_at), (rest_at, rest_tiles)])
    low_left, low_left_t, low_right = low_bases(after(left_bases, ahead[-1][1]), right_bases)
    cot = after(cot, low_left)
    rest_parts = [(0, rest_at, zyxc[::-1]), (rest_at, rest_tiles, zxyc[::-1])]
    out_plans, shapes = scatter_plans(rest_parts)
    result, mid, gmixed, d_norm, *d_rest = middle(
        me, x, positions, [part[1] for part in ahead], cot, norm_params, moments, group == seqs, w_rest, rest_plans, out_plans, shapes, rest_tiles, tile, reps, rows
    )
    result = exchange(result, "seq", group)
    if group == seqs:
        moments = result[:, :, wins * width :]
    else:
        moments = lax.all_to_all(after(moments, result), "seq", 0, 0, tiled=True)
    result = result[:, :, : wins * width].reshape(group, span, wins, width)
    result = result.transpose(0, 2, 1, 3).reshape(seq_local, span, width)
    rest_buf = scatter_tiles(d_rest, rest_parts)
    rest = cut_parts(rest_buf, rest_parts)

    qkv_total = qkv_tiles + width // tile + 1
    qkv_parts = [(0, 4, zyxc[::-1]), (4, qkv_total, zxyc[::-1])]
    out_plans, shapes = scatter_plans(qkv_parts)
    args = (w_qkv, qkv_plans, qkv_tiles, tile, reps)
    g_inputs, projs = [], []
    for w in range(wins - 1):
        qkv, _, lse = ahead[w]
        g_input, proj = attend_backward(w, me, x, positions, ids, qkv, lse, gmixed, mid, d_norm, *args)
        g_inputs.append(g_input)
        projs.append(proj)
    w = wins - 1
    qkv, _, lse = ahead[w]
    g_input, *d_qkv = attend_backward(
        w, me, x, positions, ids, qkv, lse, after(gmixed, rest_buf), mid, d_norm, *args,
        older=projs + g_inputs, out_plans=out_plans, grad_shapes=shapes, rows=rows,
    )
    steps = [[order[1 + i] for _, _, order in rest_parts] for i in range(len(orders[0]))]
    rest = [halve(buf, *step) for buf, step in zip(rest, steps[0])]
    d_qkv[-1] = after(d_qkv[-1], *rest)
    qkv_buf = scatter_tiles(d_qkv, qkv_parts)
    mine = cut_parts(qkv_buf, qkv_parts)
    for some in steps[1:]:
        rest = [halve(buf, *step, qkv_buf) for buf, step in zip(rest, some)]
    rest = join(rest, rest_parts)
    for i, some in enumerate(steps):
        mine = [halve(buf, *step, rest) for buf, step in zip(mine, some)]
    mine = join(mine, qkv_parts)
    for step in seq_bits[-2::-1]:
        rest = halve(rest, *step, mine)
        mine = halve(mine, *step, rest)
    rest, mine = rest[0], mine[0]
    g_input = jnp.stack(g_inputs + [g_input], axis=1).reshape(seq_local, span, width)
    g_input = exchange(after(g_input, result), "seq", group)

    small = mine[qkv_tiles:]
    sums = jnp.concatenate([mine[:qkv_tiles], rest], axis=0)
    tile_of = jnp.sum(
        jnp.where(owners[None, :] == jnp.arange(tiles)[:, None], jnp.arange(tiles)[None, :], 0), axis=1
    )
    sums = jnp.take(sums, tile_of, axis=0).reshape(reps, slots, rows, tile)
    sums = lax.all_to_all(after(sums, g_input), "rep", 0, 0, tiled=True)
    sums = sums.transpose(1, 0, 2, 3).reshape(slots, rows_dev, tile)

    turned = right_turn(sums, low_right, seqs)
    small = after(small, turned)
    turned = lax.all_to_all(turned, "seq", 0, 0, tiled=True)
    back = left_turns(turned, moments, low_left, low_left_t)
    back = lax.all_to_all(back, "seq", 0, 0, tiled=True)
    news = last_turn(back, low_right, *by_slot)
    first_new, second_new, new_weights = [values.transpose(1, 0, 2) for values in news]

    pos_order = zyxc
    own, other = gather(small[: width // tile], pos_order)
    masks = gather_masks(pos_order[:-1])
    table = table_of(masks + beyond(masks))
    at = jnp.arange(blocks)
    grad_pos = jnp.concatenate([own, other], axis=0)
    grad_pos = jnp.take(grad_pos, table[((at // reps) ^ me_s) * reps + ((at % reps) ^ me_r)], axis=0)
    grad_pos = grad_pos.transpose(0, 2, 1, 3).reshape(WIN, width).astype(F32)
    if aligned:
        grad_norms = small[-1, : 4 * width // tile].astype(F32)
        grad_norms = grad_norms.reshape(width // tile, 4, tile).transpose(1, 0, 2).reshape(4, width)
    else:
        grad_norms = lax.psum(d_norm, ("seq", "rep"))
    norm_first, norm_second, norm_dir = adam_step(grad_norms, norm_one, norm_two)
    pos_first, pos_second, pos_dir = adam_step(grad_pos, pos_one, pos_two)
    return (
        result,
        g_input.astype(F32),
        first_new,
        second_new,
        new_weights,
        norm_first,
        norm_second,
        norm_params - LEARN_SMALL * norm_dir,
        pos_first,
        pos_second,
        positions - LEARN_SMALL * pos_dir,
    )


def solution(mesh):
    tokens = P("rep", "seq", None)
    slots = P("seq", "rep", None)
    bases = P("rep", None, None)
    return jax.shard_map(
        body,
        mesh=mesh,
        in_specs=(
            tokens,
            tokens,
            P("rep", "seq"),
            P(),
            slots,
            bases,
            bases,
            slots,
            slots,
            P(),
            P(),
            P(),
            P(),
            P(),
            P(),
        ),
        out_specs=(tokens, tokens, slots, slots, slots, P(), P(), P(), P(), P(), P()),
        check_vma=False,
    )
```

time: 457 us -> 312 us (0.68); the launches traced: 448 us -> 308 us
  waiting for transfers between devices: 167 us -> 97.8 us
  blocking collectives: 57.3 us -> 0 us
  Pallas kernels: 62.1 us -> 93.3 us
  local copies, waits for them, and re-layouts: 45.9 us -> 19.9 us
  other arithmetic: 39.2 us -> 22 us
  matrix products: 8.74 us -> 0 us
  starting transfers between devices: 66 us -> 72.7 us
    all_to_all x9 -> x7, waiting for transfers between devices: 128 us -> 5.3 us  [the longest x1 5.29 us: body(): sums = lax.all_to_all(after(sums, g_input), 'rep', 0, 0, tiled=True)]
    all_to_all x1 -> x0, blocking collectives: 57.3 us -> none  [spread(): lax.all_to_all(jnp.broadcast_to(x[None], (size,) + x.shape), axis, 0, 0,...]
    ppermute x16 -> x38, waiting for transfers between devices: 39.4 us -> 85.6 us  [swap(): return lax.ppermute(x, axis, [(i, i ^ bit) for i in range(size)])]
    pallas_call x3 -> x10, Pallas kernels: 62.1 us -> 93.3 us  [the longest x1 29.2 us: middle(): pl.pallas_call(functools.partial(middle_kernel, plans, out_plans, reps, r...]
    unnamed x61 -> x47, local copies, waits for them, and re-layouts: 18.1 us -> 5.63 us
    ppermute x16 -> x38, starting transfers between devices: 21.7 us -> 33.2 us  [swap(): return lax.ppermute(x, axis, [(i, i ^ bit) for i in range(size)])]
    transpose x7 -> x0, other arithmetic: 10.2 us -> none  [the longest x2 5.4 us: reduce_tiles(): mine = (own + got).astype(BF).transpose(1, 0, 2, 3)]
    convert_element_type x2 -> x17, other arithmetic: 1.08 us -> 10.3 us  [the longest x13 7.57 us: add(): return (a.astype(F32) + b.astype(F32)).astype(BF)]
  transfers between devices with their start and end apart: 26 -> 46, of which waited for: 15 -> 24; matrix products, arithmetic and copies ran while one was open for 18% -> 11% of each run, Pallas kernels for 14% -> 19%
where the time goes in v2:
time: 312 us; the launch traced here: 308 us
  waiting for transfers between devices  97.8 us (31%)
  Pallas kernels  93.3 us (30%)
  starting transfers between devices  72.7 us (23%)
  other arithmetic  22 us (7%)
  local copies, waits for them, and re-layouts  19.9 us (6%)
    ppermute x38, waiting for transfers between devices, swap(): return lax.ppermute(x, axis, [(i, i ^ bit) for i in range(size)])  85.6 us
    ppermute x38, starting transfers between devices, swap(): return lax.ppermute(x, axis, [(i, i ^ bit) for i in range(size)])  33.2 us
    pallas_call x1, Pallas kernels, middle(): pl.pallas_call(functools.partial(middle_kernel, plans, out_plans, reps, r...  29.2 us
    all_to_all x5, starting transfers between devices, exchange(): return lax.all_to_all(x, axis, 0, 0, axis_index_groups=groups, tiled=True)  26.8 us
    pallas_call x2, Pallas kernels, attend_backward(): pl.pallas_call(functools.partial(attend_back_kernel, plans, out_plans, re...  23 us
    pallas_call x2, Pallas kernels, attend_forward(): pl.pallas_call(functools.partial(attend_kernel, plans, reps), grid=(1,),...  19.5 us
    convert_element_type x13, other arithmetic, add(): return (a.astype(F32) + b.astype(F32)).astype(BF)  7.57 us
    pallas_call x1, Pallas kernels, low_bases(): pl.pallas_call(bases_kernel, grid=(slots,), in_specs=[big, little], out_s...  7.3 us
  transfers between devices with their start and end apart: 46, of which 24 were waited for; matrix products, arithmetic and copies ran while one was open for 11% of the time, Pallas kernels for 19%

profile of v2, /device:TPU:0, one launch (start us, length us, event | category | flops | bytes accessed | tf_op | source)
XLA Modules:
  0.0 307.7 jit_solution(3448149355067294067)
XLA Ops:
  7.2 6.1 %all-to-all-start = ((bf16[8,64,512]{2,1,0:T(8,128)(2,1)}), bf16[8,64,512]{2,1,0:T(8,128)(2,1)S(1)}, u32[]{:S(2)}, u32[]{:S(2)}) async-start(bf16[8,64,512]{2,1,0:T(8,128)(2,1)} %get-tuple-element.136), calls=%async_computation | async-start | bytes 1048576 | tf_op jit(solution)/shard_map/all_to_all | solution.py:595
  20.5 14.2 %collective-permute-done.3 = bf16[1,7,16,256]{3,2,1,0:T(8,128)(2,1)S(1)} collective-permute-done((bf16[1,7,16,256]{3,2,1,0:T(8,128)(2,1)S(1)}, bf16[1,7,16,256]{3,2,1,0:T(8,128)(2,1)S(1)}, u32[]{:S(2)}, u32[]{:S(2)}) %collective-permute-start.3) | collective-permute-done | bytes 57376 | tf_op jit(solution)/shard_map/ppermute | solution.py:587
  46.0 3.8 %all-to-all-start.1 = ((bf16[8,64,512]{2,1,0:T(8,128)(2,1)}), bf16[8,64,512]{2,1,0:T(8,128)(2,1)S(1)}, u32[]{:S(2)}, u32[]{:S(2)}) async-start(bf16[8,64,512]{2,1,0:T(8,128)(2,1)} %get-tuple-element.70), calls=%async_computation.1 | async-start | bytes 1048576 | tf_op jit(solution)/shard_map/all_to_all | solution.py:595
  54.9 6.4 %collective-permute-done.10 = bf16[8,4,16,256]{3,2,1,0:T(8,128)(2,1)S(1)} collective-permute-done((bf16[8,4,16,256]{3,2,1,0:T(8,128)(2,1)S(1)}, bf16[8,4,16,256]{3,2,1,0:T(8,128)(2,1)S(1)}, u32[]{:S(2)}, u32[]{:S(2)}) %collective-permute-start.10) | collective-permute-done | bytes 262176 | tf_op jit(solution)/shard_map/ppermute | solution.py:587
  72.5 5.7 %all-to-all-start.2 = ((bf16[16,64,512]{2,1,0:T(8,128)(2,1)}), bf16[16,64,512]{2,1,0:T(8,128)(2,1)S(1)}, u32[]{:S(2)}, u32[]{:S(2)}) async-start(bf16[16,64,512]{2,1,0:T(8,128)(2,1)} %param.20), calls=%async_computation.2 | async-start | bytes 2097152 | tf_op jit(solution)/shard_map/all_to_all | solution.py:595
  78.3 9.7 %attend_forward.2 = (bf16[1,512,1536]{2,1,0:T(8,128)(2,1)}, bf16[1,512,512]{2,1,0:T(8,128)(2,1)}, f32[1,8,512]{2,1,0:T(8,128)}) custom-call(s32[2]{0:T(128)} %pad_add_fusion.me_ref, bf16[8,64,512]{2,1,0:T(8,128)(2,1)} %copy-done.11, f32[512,512]{1,0:T(8,128)} %pos_ref.9, s32[2,1,512]{2,1,0:T(1,128)} %copy.50.ids_row, s32[2,512,1]{2,1,0:T(8,128)} %copy.51.ids_col, ...), custom_call_target="tpu_custom_call" | custom-call | flops 8800000000 | tf_op jit(solution)/shard_map/attend_forward/pallas_call | solution.py:167
  94.5 9.8 %attend_forward.3 = (bf16[1,512,1536]{2,1,0:T(8,128)(2,1)}, bf16[1,512,512]{2,1,0:T(8,128)(2,1)}, f32[1,8,512]{2,1,0:T(8,128)}) custom-call(s32[2]{0:T(128)} %pad_add_fusion.me_ref, bf16[8,64,512]{2,1,0:T(8,128)(2,1)} %copy-done.12, f32[512,512]{1,0:T(8,128)} %pos_ref.9, s32[2,1,512]{2,1,0:T(1,128)} %broadcast_in_dim.77.ids_row, s32[2,512,1]{2,1,0:T(8,128)} %copy.52.ids_col, ...), custom_call_target="tpu_custom_call" | custom-call | flops 8800000000 | tf_op jit(solution)/shard_map/attend_forward/pallas_call | solution.py:167
  104.3 7.3 %low_bases.1 = (bf16[6,512,512]{2,1,0:T(8,128)(2,1)}, bf16[6,512,512]{2,1,0:T(8,128)(2,1)}, bf16[6,256,256]{2,1,0:T(8,128)(2,1)}) custom-call(f32[6,512,512]{2,1,0:T(8,128)} %left_ref, f32[6,256,256]{2,1,0:T(8,128)} %right_ref.1), custom_call_target="tpu_custom_call" | custom-call | tf_op jit(solution)/shard_map/low_bases/pallas_call | solution.py:570
  112.5 29.2 %middle.1 = (bf16[8,64,1408]{2,1,0:T(8,128)(2,1)}, f32[2,512,512]{2,1,0:T(8,128)}, bf16[2,512,512]{2,1,0:T(8,128)(2,1)}, f32[4,512]{1,0:T(4,128)}, bf16[288,16,2...) custom-call(s32[2]{0:T(128)} %pad_add_fusion.me_ref, f32[512,512]{1,0:T(8,128)} %pos_ref.9, ...), custom_call_target="tpu_custom_call" | custom-call | flops 29699999744 | tf_op jit(solution)/shard_map/middle/pallas_call | solution.py:299
  142.7 6.1 %all-to-all-start.3 = ((bf16[8,64,1408]{2,1,0:T(8,128)(2,1)}), bf16[8,64,1408]{2,1,0:T(8,128)(2,1)S(1)}, u32[]{:S(2)}, u32[]{:S(2)}) async-start(bf16[8,64,1408]{2,1,0:T(8,128)(2,1)} %get-tuple-element.87), calls=%async_computation.3 | async-start | bytes 2883584 | tf_op jit(solution)/shard_map/all_to_all | solution.py:595
  148.8 9.7 %attend_backward.2 = (bf16[8,64,512]{2,1,0:T(8,128)(2,1)}, bf16[512,1536]{1,0:T(8,128)(2,1)}) custom-call(s32[2]{0:T(128)} %pad_add_fusion.me_ref, bf16[8,64,512]{2,1,0:T(8,128)(2,1)} %copy-done.11, f32[512,512]{1,0:T(8,128)} %pos_ref.9, s32[2,1,512]{2,1,0:T(1,128)} %broadcast_in_dim.77.ids_row, s32[2,512,1]{2,1,0:T(8,128)} %copy.52.ids_col, ...), custom_call_target="tpu_custom_call" | custom-call | flops 11000000512 | tf_op jit(solution)/shard_map/attend_backward/pallas_call | solution.py:438
  165.3 13.3 %attend_backward.3 = (bf16[8,64,512]{2,1,0:T(8,128)(2,1)}, bf16[144,16,256]{2,1,0:T(8,128)(2,1)}, bf16[144,16,256]{2,1,0:T(8,128)(2,1)}) custom-call(s32[2]{0:T(128)} %pad_add_fusion.me_ref, bf16[8,64,512]{2,1,0:T(8,128)(2,1)} %copy-done.12, f32[512,512]{1,0:T(8,128)} %pos_ref.9, s32[2,1,512]{2,1,0:T(1,128)} %broadcast_in_dim.77.ids_row, ...), custom_call_target="tpu_custom_call" | custom-call | flops 11000000512 | tf_op jit(solution)/shard_map/attend_backward/pallas_call | solution.py:438
  178.6 5.5 %collective-permute-done.21 = bf16[72,16,256]{2,1,0:T(8,128)(2,1)} collective-permute-done((bf16[72,16,256]{2,1,0:T(8,128)(2,1)S(1)}, bf16[72,16,256]{2,1,0:T(8,128)(2,1)}, u32[]{:S(2)}, u32[]{:S(2)}) %collective-permute-start.21) | collective-permute-done | bytes 589856 | tf_op jit(solution)/shard_map/ppermute | solution.py:587
  188.8 5.2 %all-to-all-start.4 = ((bf16[16,64,512]{2,1,0:T(8,128)(2,1)}), bf16[16,64,512]{2,1,0:T(8,128)(2,1)S(1)}, u32[]{:S(2)}, u32[]{:S(2)}) async-start(bf16[16,64,512]{2,1,0:T(8,128)(2,1)} %bitcast.27), calls=%async_computation.4 | async-start | bytes 2097152 | tf_op jit(solution)/shard_map/all_to_all | solution.py:595
  199.4 4.8 %collective-permute-done.25 = bf16[36,16,256]{2,1,0:T(8,128)(2,1)S(1)} collective-permute-done((bf16[36,16,256]{2,1,0:T(8,128)(2,1)S(1)}, bf16[36,16,256]{2,1,0:T(8,128)(2,1)S(1)}, u32[]{:S(2)}, u32[]{:S(2)}) %collective-permute-start.25) | collective-permute-done | bytes 294944 | tf_op jit(solution)/shard_map/ppermute | solution.py:587
  204.3 10.0 %collective-permute-done.24 = bf16[36,16,256]{2,1,0:T(8,128)(2,1)S(1)} collective-permute-done((bf16[36,16,256]{2,1,0:T(8,128)(2,1)S(1)}, bf16[36,16,256]{2,1,0:T(8,128)(2,1)S(1)}, u32[]{:S(2)}, u32[]{:S(2)}) %collective-permute-start.24) | collective-permute-done | bytes 294944 | tf_op jit(solution)/shard_map/ppermute | solution.py:587
  221.2 5.5 %collective-permute-done.30 = bf16[2,18,16,256]{3,2,1,0:T(8,128)(2,1)S(1)} collective-permute-done((bf16[2,18,16,256]{3,2,1,0:T(8,128)(2,1)S(1)}, bf16[2,18,16,256]{3,2,1,0:T(8,128)(2,1)S(1)}, u32[]{:S(2)}, u32[]{:S(2)}) %collective-permute-start.30) | collective-permute-done | bytes 294944 | tf_op jit(solution)/shard_map/ppermute | solution.py:587
  227.5 5.5 %collective-permute-done.28 = bf16[20,16,256]{2,1,0:T(8,128)(2,1)S(1)} collective-permute-done((bf16[20,16,256]{2,1,0:T(8,128)(2,1)S(1)}, bf16[20,16,256]{2,1,0:T(8,128)(2,1)S(1)}, u32[]{:S(2)}, u32[]{:S(2)}) %collective-permute-start.28) | collective-permute-done | bytes 163872 | tf_op jit(solution)/shard_map/ppermute | solution.py:587
  236.1 4.6 %collective-permute-done.29 = bf16[2,9,16,256]{3,2,1,0:T(8,128)(2,1)S(1)} collective-permute-done((bf16[2,9,16,256]{3,2,1,0:T(8,128)(2,1)S(1)}, bf16[2,9,16,256]{3,2,1,0:T(8,128)(2,1)S(1)}, u32[]{:S(2)}, u32[]{:S(2)}) %collective-permute-start.29) | collective-permute-done | bytes 147488 | tf_op jit(solution)/shard_map/ppermute | solution.py:587
  250.9 5.3 %all-to-all-done.5 = bf16[4,6,16,256]{3,2,1,0:T(8,128)(2,1)S(1)} async-done(((bf16[4,6,16,256]{3,2,1,0:T(8,128)(2,1)}), bf16[4,6,16,256]{3,2,1,0:T(8,128)(2,1)S(1)}, u32[]{:S(2)}, u32[]{:S(2)}) %all-to-all-start.5) | async-done | bytes 196640 | tf_op jit(solution)/shard_map/all_to_all | solution.py:849
  273.5 4.1 %collective-permute-done.36 = bf16[8,2,16,256]{3,2,1,0:T(8,128)(2,1)S(1)} collective-permute-done((bf16[8,2,16,256]{3,2,1,0:T(8,128)(2,1)S(1)}, bf16[8,2,16,256]{3,2,1,0:T(8,128)(2,1)S(1)}, u32[]{:S(2)}, u32[]{:S(2)}) %collective-permute-start.36) | collective-permute-done | bytes 131104 | tf_op jit(solution)/shard_map/ppermute | solution.py:587
  279.1 6.2 %left_turns.1 = bf16[8,64,384]{2,1,0:T(8,128)(2,1)} custom-call(bf16[8,64,192]{2,1,0:T(8,128)(2,1)} %copy-done.9, bf16[8,64,384]{2,1,0:T(8,128)(2,1)} %slice.254.moments_ref, bf16[6,512,512]{2,1,0:T(8,128)(2,1)} %get-tuple-element.85.left_ref, bf16[6,512,512]{2,1,0:T(8,128)(2,1)} %get-tuple-element.117.left_t_ref), custom_call_target="tpu_custom_call" | custom-call | tf_op jit(solution)/shard_map/left_turns/pallas_call | solution.py:500
  285.3 5.9 %all-to-all-start.7 = ((bf16[8,64,384]{2,1,0:T(8,128)(2,1)}), bf16[8,64,384]{2,1,0:T(8,128)(2,1)S(1)}, u32[]{:S(2)}, u32[]{:S(2)}) async-start(bf16[8,64,384]{2,1,0:T(8,128)(2,1)} %left_turns.1), calls=%async_computation.7 | async-start | bytes 786432 | tf_op jit(solution)/shard_map/all_to_all | solution.py:856
  296.6 6.8 %all-to-all-done.7.back_ref = bf16[8,64,384]{2,1,0:T(8,128)(2,1)S(1)} async-done(((bf16[8,64,384]{2,1,0:T(8,128)(2,1)}), bf16[8,64,384]{2,1,0:T(8,128)(2,1)S(1)}, u32[]{:S(2)}, u32[]{:S(2)}) %all-to-all-start.7) | async-done | bytes 393248 | tf_op jit(solution)/shard_map/all_to_all | solution.py:856
  (233 shorter events, 115.0 us)
Async XLA Ops:
  1.7 12.4 %collective-permute-start = (bf16[6,16,256]{2,1,0:T(8,128)(2,1)S(1)}, bf16[6,16,256]{2,1,0:T(8,128)(2,1)S(1)}, u32[]{:S(2)}, u32[]{:S(2)}) collective-permute-start(bf16[6,16,256]{2,1,0:T(8,128)(2,1)S(1)} %get-tuple-element.145), channel_id=1, source_target_pairs={{0,1},{1,0},{2,3},{3,2},{4,5},{5,4},{6,7},{7,6},{8,9},{9,8},{10,11... | collective-permute-start | bytes 147464 | tf_op jit(solution)/shard_map/ppermute | solution.py:587
  2.2 11.9 %collective-permute-start.1 = (bf16[6,16,256]{2,1,0:T(8,128)(2,1)S(1)}, bf16[6,16,256]{2,1,0:T(8,128)(2,1)S(1)}, u32[]{:S(2)}, u32[]{:S(2)}) collective-permute-start(bf16[6,16,256]{2,1,0:T(8,128)(2,1)S(1)} %get-tuple-element.144), channel_id=1, source_target_pairs={{0,2},{1,3},{2,0},{3,1},{4,6},{5,7},{6,4},{7,5},{8,10},{9,11},{10,... | collective-permute-start | bytes 147464 | tf_op jit(solution)/shard_map/ppermute | solution.py:587
  7.2 33.2 %all-to-all-start = ((bf16[8,64,512]{2,1,0:T(8,128)(2,1)}), bf16[8,64,512]{2,1,0:T(8,128)(2,1)S(1)}, u32[]{:S(2)}, u32[]{:S(2)}) async-start(bf16[8,64,512]{2,1,0:T(8,128)(2,1)} %get-tuple-element.136), calls=%async_computation | async-start | bytes 1048576 | tf_op jit(solution)/shard_map/all_to_all | solution.py:595
  14.9 19.8 %collective-permute-start.3 = (bf16[1,7,16,256]{3,2,1,0:T(8,128)(2,1)S(1)}, bf16[1,7,16,256]{3,2,1,0:T(8,128)(2,1)S(1)}, u32[]{:S(2)}, u32[]{:S(2)}) collective-permute-start(bf16[1,7,16,256]{3,2,1,0:T(8,128)(2,1)S(1)} %maximum_bitcast_fusion), channel_id=1, source_target_pairs={{0,16},{4,20},{8,24},{12,28},{16,0},{20,4},{24,8},{28,12},{1,17},{... | collective-permute-start | bytes 172040 | tf_op jit(solution)/shard_map/ppermute | solution.py:587
  20.5 16.7 %collective-permute-start.6 = (bf16[1,18,16,256]{3,2,1,0:T(8,128)(2,1)S(1)}, bf16[1,18,16,256]{3,2,1,0:T(8,128)(2,1)S(1)}, u32[]{:S(2)}, u32[]{:S(2)}) collective-permute-start(bf16[1,18,16,256]{3,2,1,0:T(8,128)(2,1)S(1)} %slice_bitcast_fusion.2), channel_id=1, source_target_pairs={{0,16},{4,20},{8,24},{12,28},{16,0},{20,4},{24,8},{28,12},{1,17},{... | collective-permute-start | bytes 442376 | tf_op jit(solution)/shard_map/ppermute | solution.py:587
  46.0 25.7 %all-to-all-start.1 = ((bf16[8,64,512]{2,1,0:T(8,128)(2,1)}), bf16[8,64,512]{2,1,0:T(8,128)(2,1)S(1)}, u32[]{:S(2)}, u32[]{:S(2)}) async-start(bf16[8,64,512]{2,1,0:T(8,128)(2,1)} %get-tuple-element.70), calls=%async_computation.1 | async-start | bytes 1048576 | tf_op jit(solution)/shard_map/all_to_all | solution.py:595
  49.8 13.2 %collective-permute-start.11 = (bf16[8,3,16,256]{3,2,1,0:T(8,128)(2,1)S(1)}, bf16[8,3,16,256]{3,2,1,0:T(8,128)(2,1)S(1)}, u32[]{:S(2)}, u32[]{:S(2)}) collective-permute-start(bf16[8,3,16,256]{3,2,1,0:T(8,128)(2,1)S(1)} %pad_maximum_fusion.15), channel_id=1, source_target_pairs={{0,4},{4,0},{8,12},{12,8},{16,20},{20,16},{24,28},{28,24},{1,5},{5... | collective-permute-start | bytes 589832 | tf_op jit(solution)/shard_map/ppermute | solution.py:587
  54.1 13.4 %collective-permute-start.9 = (bf16[4,9,16,256]{3,2,1,0:T(8,128)(2,1)S(1)}, bf16[4,9,16,256]{3,2,1,0:T(8,128)(2,1)S(1)}, u32[]{:S(2)}, u32[]{:S(2)}) collective-permute-start(bf16[4,9,16,256]{3,2,1,0:T(8,128)(2,1)S(1)} %get-tuple-element.139), channel_id=1, source_target_pairs={{0,4},{4,0},{8,12},{12,8},{16,20},{20,16},{24,28},{28,24},{1,5},{5... | collective-permute-start | bytes 884744 | tf_op jit(solution)/shard_map/ppermute | solution.py:587
  62.1 16.2 %collective-permute-start.14 = (bf16[16,4,16,256]{3,2,1,0:T(8,128)(2,1)}, bf16[16,4,16,256]{3,2,1,0:T(8,128)(2,1)}, u32[]{:S(2)}, u32[]{:S(2)}) collective-permute-start(bf16[16,4,16,256]{3,2,1,0:T(8,128)(2,1)} %pad_maximum_fusion.8.refs_0_), channel_id=1, source_target_pairs={{0,1},{1,0},{2,3},{3,2},{4,5},{5,4},{6,7},{7,6},{8,9},{9,8},{10,11... | collective-permute-start | bytes 1572872 | tf_op jit(solution)/shard_map/ppermute | solution.py:587
  63.8 14.4 %collective-permute-start.15 = (bf16[16,3,16,256]{3,2,1,0:T(8,128)(2,1)}, bf16[16,3,16,256]{3,2,1,0:T(8,128)(2,1)}, u32[]{:S(2)}, u32[]{:S(2)}) collective-permute-start(bf16[16,3,16,256]{3,2,1,0:T(8,128)(2,1)} %pad_maximum_fusion.9.refs_2_), channel_id=1, source_target_pairs={{0,1},{1,0},{2,3},{3,2},{4,5},{5,4},{6,7},{7,6},{8,9},{9,8},{10,11... | collective-permute-start | bytes 1179656 | tf_op jit(solution)/shard_map/ppermute | solution.py:587
  67.6 20.9 %collective-permute-start.16 = (bf16[8,9,16,256]{3,2,1,0:T(8,128)(2,1)S(1)}, bf16[8,9,16,256]{3,2,1,0:T(8,128)(2,1)}, u32[]{:S(2)}, u32[]{:S(2)}) collective-permute-start(bf16[8,9,16,256]{3,2,1,0:T(8,128)(2,1)S(1)} %pad_maximum_fusion.7), channel_id=1, source_target_pairs={{0,4},{4,0},{8,12},{12,8},{16,20},{20,16},{24,28},{28,24},{1,5},{5... | collective-permute-start | bytes 1769480 | tf_op jit(solution)/shard_map/ppermute | solution.py:587
  68.5 20.0 %collective-permute-start.13 = (bf16[8,9,16,256]{3,2,1,0:T(8,128)(2,1)S(1)}, bf16[8,9,16,256]{3,2,1,0:T(8,128)(2,1)}, u32[]{:S(2)}, u32[]{:S(2)}) collective-permute-start(bf16[8,9,16,256]{3,2,1,0:T(8,128)(2,1)S(1)} %pad_maximum_fusion.6), channel_id=1, source_target_pairs={{0,2},{1,3},{2,0},{3,1},{4,6},{5,7},{6,4},{7,5},{8,10},{9,11},{10,... | collective-permute-start | bytes 1769480 | tf_op jit(solution)/shard_map/ppermute | solution.py:587
  72.5 39.1 %all-to-all-start.2 = ((bf16[16,64,512]{2,1,0:T(8,128)(2,1)}), bf16[16,64,512]{2,1,0:T(8,128)(2,1)S(1)}, u32[]{:S(2)}, u32[]{:S(2)}) async-start(bf16[16,64,512]{2,1,0:T(8,128)(2,1)} %param.20), calls=%async_computation.2 | async-start | bytes 2097152 | tf_op jit(solution)/shard_map/all_to_all | solution.py:595
  92.3 19.3 %collective-permute-start.18 = (bf16[16,9,16,256]{3,2,1,0:T(8,128)(2,1)S(1)}, bf16[16,9,16,256]{3,2,1,0:T(8,128)(2,1)}, u32[]{:S(2)}, u32[]{:S(2)}) collective-permute-start(bf16[16,9,16,256]{3,2,1,0:T(8,128)(2,1)S(1)} %pad_maximum_fusion.1.refs_6_), channel_id=1, source_target_pairs={{0,1},{1,0},{2,3},{3,2},{4,5},{5,4},{6,7},{7,6},{8,9},{9,8},{10,11... | collective-permute-start | bytes 3538952 | tf_op jit(solution)/shard_map/ppermute | solution.py:587
  92.3 19.3 %collective-permute-start.17 = (bf16[16,9,16,256]{3,2,1,0:T(8,128)(2,1)}, bf16[16,9,16,256]{3,2,1,0:T(8,128)(2,1)}, u32[]{:S(2)}, u32[]{:S(2)}) collective-permute-start(bf16[16,9,16,256]{3,2,1,0:T(8,128)(2,1)} %pad_maximum_fusion.refs_4_), channel_id=1, source_target_pairs={{0,1},{1,0},{2,3},{3,2},{4,5},{5,4},{6,7},{7,6},{8,9},{9,8},{10,11... | collective-permute-start | bytes 3538952 | tf_op jit(solution)/shard_map/ppermute | solution.py:587
  141.8 16.8 %collective-permute-start.19 = (bf16[288,16,256]{2,1,0:T(8,128)(2,1)}, bf16[288,16,256]{2,1,0:T(8,128)(2,1)}, u32[]{:S(2)}, u32[]{:S(2)}) collective-permute-start(bf16[288,16,256]{2,1,0:T(8,128)(2,1)} %get-tuple-element.97), channel_id=1, source_target_pairs={{0,1},{1,0},{2,3},{3,2},{4,5},{5,4},{6,7},{7,6},{8,9},{9,8},{10,11... | collective-permute-start | bytes 7077896 | tf_op jit(solution)/shard_map/ppermute | solution.py:587
  142.7 44.9 %all-to-all-start.3 = ((bf16[8,64,1408]{2,1,0:T(8,128)(2,1)}), bf16[8,64,1408]{2,1,0:T(8,128)(2,1)S(1)}, u32[]{:S(2)}, u32[]{:S(2)}) async-start(bf16[8,64,1408]{2,1,0:T(8,128)(2,1)} %get-tuple-element.87), calls=%async_computation.3 | async-start | bytes 2883584 | tf_op jit(solution)/shard_map/all_to_all | solution.py:595
  161.7 16.8 %collective-permute-start.20 = (bf16[72,16,256]{2,1,0:T(8,128)(2,1)S(1)}, bf16[72,16,256]{2,1,0:T(8,128)(2,1)S(1)}, u32[]{:S(2)}, u32[]{:S(2)}) collective-permute-start(bf16[72,16,256]{2,1,0:T(8,128)(2,1)S(1)} %get-tuple-element.133), channel_id=1, source_target_pairs={{0,2},{1,3},{2,0},{3,1},{4,6},{5,7},{6,4},{7,5},{8,10},{9,11},{10,... | collective-permute-start | bytes 1769480 | tf_op jit(solution)/shard_map/ppermute | solution.py:587
  163.3 20.8 %collective-permute-start.21 = (bf16[72,16,256]{2,1,0:T(8,128)(2,1)S(1)}, bf16[72,16,256]{2,1,0:T(8,128)(2,1)}, u32[]{:S(2)}, u32[]{:S(2)}) collective-permute-start(bf16[72,16,256]{2,1,0:T(8,128)(2,1)S(1)} %get-tuple-element.132), channel_id=1, source_target_pairs={{0,4},{4,0},{8,12},{12,8},{16,20},{20,16},{24,28},{28,24},{1,5},{5... | collective-permute-start | bytes 1769480 | tf_op jit(solution)/shard_map/ppermute | solution.py:587
  188.8 58.7 %all-to-all-start.4 = ((bf16[16,64,512]{2,1,0:T(8,128)(2,1)}), bf16[16,64,512]{2,1,0:T(8,128)(2,1)S(1)}, u32[]{:S(2)}, u32[]{:S(2)}) async-start(bf16[16,64,512]{2,1,0:T(8,128)(2,1)} %bitcast.27), calls=%async_computation.4 | async-start | bytes 2097152 | tf_op jit(solution)/shard_map/all_to_all | solution.py:595
  195.7 18.7 %collective-permute-start.24 = (bf16[36,16,256]{2,1,0:T(8,128)(2,1)S(1)}, bf16[36,16,256]{2,1,0:T(8,128)(2,1)S(1)}, u32[]{:S(2)}, u32[]{:S(2)}) collective-permute-start(bf16[36,16,256]{2,1,0:T(8,128)(2,1)S(1)} %slice.232), channel_id=1, source_target_pairs={{0,4},{4,0},{8,12},{12,8},{16,20},{20,16},{24,28},{28,24},{1,5},{5... | collective-permute-start | bytes 884744 | tf_op jit(solution)/shard_map/ppermute | solution.py:587
  264.1 14.3 %all-to-all-start.6 = ((bf16[8,64,192]{2,1,0:T(8,128)(2,1)}), bf16[8,64,192]{2,1,0:T(8,128)(2,1)S(1)}, u32[]{:S(2)}, u32[]{:S(2)}) async-start(bf16[8,64,192]{2,1,0:T(8,128)(2,1)} %right_turn.1), calls=%async_computation.6 | async-start | bytes 524288 | tf_op jit(solution)/shard_map/all_to_all | solution.py:854
  277.6 13.6 %collective-permute-start.37 = (bf16[16,2,16,256]{3,2,1,0:T(8,128)(2,1)S(1)}, bf16[16,2,16,256]{3,2,1,0:T(8,128)(2,1)S(1)}, u32[]{:S(2)}, u32[]{:S(2)}) collective-permute-start(bf16[16,2,16,256]{3,2,1,0:T(8,128)(2,1)S(1)} %get-tuple-element.146), channel_id=1, source_target_pairs={{0,1},{1,0},{2,3},{3,2},{4,5},{5,4},{6,7},{7,6},{8,9},{9,8},{10,11... | collective-permute-start | bytes 786440 | tf_op jit(solution)/shard_map/ppermute | solution.py:587
  285.3 18.1 %all-to-all-start.7 = ((bf16[8,64,384]{2,1,0:T(8,128)(2,1)}), bf16[8,64,384]{2,1,0:T(8,128)(2,1)S(1)}, u32[]{:S(2)}, u32[]{:S(2)}) async-start(bf16[8,64,384]{2,1,0:T(8,128)(2,1)} %left_turns.1), calls=%async_computation.7 | async-start | bytes 786432 | tf_op jit(solution)/shard_map/all_to_all | solution.py:856
  (42 other events, 317.4 us)
